TPU v7x, 32 devices: a whole 2x2x4 slice. The times are simulated.
32 devices in a mesh: dp: 8 (over z, y), head: 4 (over x, core).
Axes of the slice: x: 2, y: 2, z: 4, core: 2. Of those that a mesh axis runs over, the one named last changes fastest.
Arguments:
- latent: bfloat16 [12288, 512], P('dp', 'head'), may hold values from -6 to 6
- value_grad: bfloat16 [12288, 2048], P('dp', 'head'), may hold values from -6 to 6
- lengths: int32 [8], replicated, may hold values from 1 to 1536, 4096 in all
Outputs:
- update: bfloat16 [16, 512, 128], P('head')
Inputs may be any that keep to these rules, and one draw needn't show every extreme that they name: The lengths sum to 4096; the longest is exactly 1536.
All inputs are finite; a program needn't handle non-finite values.
Results may differ from a plain program's by a relative error of at most 0.035.
Values may be sent and summed in bfloat16 or wider, within the bound.
A program may use at most 64 MiB of HBM per device.

v0:
```python
import jax
import jax.numpy as jnp
from jax import lax
from jax.sharding import PartitionSpec as P

KV_RANK = 512
V_DIM = 128
ITERS = 5


epsilon = 1e-07
coef_one = 3.4445
coef_two = -4.775
coef_three = 2.0315


def body(latent, value_grad, lengths):
    capacity, lat_cols = latent.shape
    grad_width = value_grad.shape[1]
    head_count = grad_width // V_DIM
    my_index = lax.axis_index("dp")
    own_length = lengths[my_index]
    slot_live = jnp.arange(capacity, dtype=jnp.int32) < own_length
    rows_grad = jnp.where(slot_live[:, None], value_grad, jnp.zeros_like(value_grad))
    partial_sum = lax.dot_general(
        lax.all_gather(latent, "head", axis=1, tiled=True),
        rows_grad,
        (((0,), (0,)), ((), ())),
        preferred_element_type=jnp.float32,
    )
    dw_shard = lax.psum_scatter(partial_sum, "dp", scatter_dimension=0, tiled=True)
    shard_heads = dw_shard.reshape(dw_shard.shape[0], head_count, V_DIM)
    local_squares = jnp.sum(shard_heads * shard_heads, axis=(0, 2))
    square_total = lax.psum(local_squares, "dp")
    head_norm = jnp.sqrt(square_total)
    ortho_shard = (shard_heads / (head_norm[None, :, None] + epsilon)).astype(jnp.bfloat16)
    ortho = lax.all_gather(ortho_shard, "dp", axis=0, tiled=True)
    for step in range(ITERS):
        gram_mat = jnp.einsum(
            "rhv,rhw->hvw", ortho, ortho, preferred_element_type=jnp.float32
        ).astype(jnp.bfloat16)
        squared = jnp.einsum("hvu,huw->hvw", gram_mat, gram_mat, preferred_element_type=jnp.float32)
        poly_mat = (coef_two * gram_mat.astype(jnp.float32) + coef_three * squared).astype(
            jnp.bfloat16
        )
        product = jnp.einsum("rhv,hvw->rhw", ortho, poly_mat, preferred_element_type=jnp.float32)
        ortho = (coef_one * ortho.astype(jnp.float32) + product).astype(jnp.bfloat16)
    scale = 0.2 * max(KV_RANK, V_DIM) ** 0.5
    update = (scale * ortho.astype(jnp.float32)).astype(jnp.bfloat16)
    return jnp.transpose(update, (1, 0, 2))


def solution(mesh):
    return jax.shard_map(
        body,
        mesh=mesh,
        in_specs=(P("dp", "head"), P("dp", "head"), P()),
        out_specs=P("head", None, None),
        check_vma=False,
    )
```

profile of v0, /device:TPU:0, one launch (start us, length us, event | category | flops | bytes accessed | tf_op | source)
XLA Modules:
  0.0 163.9 jit_solution(18217347947089124987)
XLA Ops:
  6.5 0.7 all-gather.2.cloned.1.call-update
  7.3 1.2 dynamic_slice.3
  8.5 0.7 iota_compare_fusion
  9.2 22.3 %all-gather.2.cloned.1.call-done = bf16[1536,512]{1,0:T(8,128)(2,1)} async-done(((bf16[1536,128]{1,0:T(8,128)(2,1)}), bf16[1536,512]{1,0:T(8,128)(2,1)}) %all-gather.2.cloned.1.call-update) | async-done | bytes 1572880 | tf_op jit(solution)/shard_map/all_gather | solution.py:26
  31.5 3.0 %fusion.3 = f32[512,512]{0,1:T(8,128)S(1)} fusion(bf16[1536,512]{1,0:T(8,128)(2,1)} %all-gather.2.cloned.1.call-done, bf16[1536,512]{1,0:T(8,128)(2,1)} %param.4, pred[1536]{0:T(1024)(128)(4,1)S(1)} %iota_compare_fusion), kind=kOutput, calls=%fused_computation.3 | convolution fusion | flops 806092800 | bytes 4195840 | tf_op jit(solution)/shard_map/dot_general | solution.py:25
  34.5 1.3 copy.81
  35.8 63.9 %reduce-scatter.4.cloned.1.call-done = f32[64,512]{1,0:T(8,128)} async-done(((f32[512,512]{1,0:T(8,128)}), f32[64,512]{1,0:T(8,128)}) %reduce-scatter.4.cloned.1.call-update) | async-done | bytes 131088
  99.7 1.0 copy.82
  100.8 0.1 multiply_reduce_fusion
  100.9 0.1 bitcast_reduce_fusion
  101.0 19.5 %psum.7 = f32[4]{0:T(128)S(1)} all-reduce(f32[4]{0:T(128)S(1)} %bitcast_reduce_fusion), channel_id=1, replica_groups=mesh['dp'=8,'head'=4] {'dp'}, use_global_device_ids=true, to_apply=%region_3.4 | all-reduce | flops 4 | bytes 32 | tf_op jit(solution)/shard_map/psum | solution.py:34
  120.5 0.1 copy.50
  120.6 0.1 divide_convert_fusion
  120.7 31.6 %all_gather.7 = bf16[512,4,128]{2,0,1:T(8,128)(2,1)S(1)} all-gather(bf16[64,4,128]{2,0,1:T(8,128)(2,1)S(1)} %divide_convert_fusion), channel_id=1, replica_groups=mesh['dp'=8,'head'=4] {'dp'}, dimensions={0}, use_global_device_ids=true | all-gather | bytes 589824 | tf_op jit(solution)/shard_map/all_gather | solution.py:37
  152.3 0.3 convolution_convert_fusion.4
  152.7 0.4 fusion.11
  153.1 0.4 convolution_convert_fusion.3
  153.5 0.4 fusion.12
  153.9 0.4 convolution_convert_fusion.2
  154.3 0.4 fusion.13
  154.7 0.4 convolution_convert_fusion.1
  155.0 0.4 fusion.14
  155.5 0.4 convolution_convert_fusion
  155.8 1.2 fusion.19
  (4 shorter events, 0.1 us)
Async XLA Ops:
  6.5 24.9 %all-gather.2.cloned.1.call-start = ((), (), s32[]{:S(2)}) async-start(), calls=%async_computation.1 | async-start | bytes 1966080 | tf_op jit(solution)/shard_map/all_gather | solution.py:26
  7.3 92.5 %reduce-scatter.4.cloned.1.call-start = ((), (), s32[]{:S(2)}) async-start(), calls=%async_computation.2 | async-start | bytes 1179648
Sparse Core Ops, SparseCore 0:
  8.9 22.5 all-gather.1
  35.9 63.7 reduce-scatter.3
where the time goes:
time: 164 us
  waiting for transfers between devices  86.9 us (53%)
  blocking collectives  51.1 us (31%)
  between operations  13.5 us (8%)
  matrix products  7.7 us (5%)
  local copies, waits for them, and re-layouts  3.71 us (2%)
    unnamed x3, waiting for transfers between devices  64.6 us
    all_gather x1, blocking collectives, body(): ortho = lax.all_gather(ortho_shard, 'dp', axis=0, tiled=True)  31.6 us
    all_gather x1, waiting for transfers between devices, body(): lax.all_gather(latent, 'head', axis=1, tiled=True)  22.3 us
    psum x1, blocking collectives, body(): square_total = lax.psum(local_squares, 'dp')  19.5 us
  transfers between devices with their start and end apart: 2, of which 2 were waited for; matrix products, arithmetic and copies ran while one was open for 1% of the time, Pallas kernels for 0%

commit v1 on v0

--- a/solution.py
+++ b/solution.py
@@ -1,12 +1,17 @@
+import functools
+
 import jax
 import jax.numpy as jnp
 from jax import lax
+from jax.experimental import pallas as pl
+from jax.experimental.pallas import tpu as pltpu
 from jax.sharding import PartitionSpec as P
 
 KV_RANK = 512
 V_DIM = 128
 ITERS = 5
-
+TILE = 16
+CHUNKS = 3
 
 epsilon = 1e-07
 coef_one = 3.4445
@@ -14,7 +19,7 @@
 coef_three = 2.0315
 
 
-def body(latent, value_grad, lengths):
+def plain_body(latent, value_grad, lengths):
     capacity, lat_cols = latent.shape
     grad_width = value_grad.shape[1]
     head_count = grad_width // V_DIM
@@ -50,7 +55,200 @@
     return jnp.transpose(update, (1, 0, 2))
 
 
+def dot_f32(a, b, dims):
+    return lax.dot_general(a, b, (dims, ((), ())), preferred_element_type=jnp.float32)
+
+
+def newton_schulz(grads):
+    final = 0.2 * max(KV_RANK, V_DIM) ** 0.5
+    xs = list(grads)
+    inv = []
+    for g in xs:
+        w = g.astype(jnp.float32)
+        rows = jnp.sum(w * w, axis=0, keepdims=True)
+        inv.append(1.0 / (jnp.sqrt(jnp.sum(rows, axis=1, keepdims=True)) + epsilon))
+    for step in range(ITERS):
+        grams = [dot_f32(x, x, ((0,), (0,))) for x in xs]
+        if step == 0:
+            grams = [a * s * s for a, s in zip(grams, inv)]
+        grams = [a.astype(jnp.bfloat16) for a in grams]
+        squares = [dot_f32(a, a, ((1,), (0,))) for a in grams]
+        polys = [
+            (coef_two * a.astype(jnp.float32) + coef_three * q).astype(jnp.bfloat16)
+            for a, q in zip(grams, squares)
+        ]
+        prods = [dot_f32(x, b, ((1,), (0,))) for x, b in zip(xs, polys)]
+        wide = [coef_one * x.astype(jnp.float32) + p for x, p in zip(xs, prods)]
+        if step == 0:
+            wide = [x * s for x, s in zip(wide, inv)]
+        xs = [x.astype(jnp.bfloat16) for x in wide]
+    return [(final * x.astype(jnp.float32)).astype(jnp.bfloat16) for x in xs]
+
+
+def kernel(
+    n_dp,
+    len_ref, lat_hbm, vg_hbm, out_ref,
+    lat_v, vg_v, lat_t, acc, part, rs_buf, grad,
+    load_sem, sib_sem, x_send, x_recv, f_send, f_recv, rs_send, rs_recv, ag_send, ag_recv,
+):
+    dp = lax.axis_index("dp")
+    head = lax.axis_index("head")
+    core = lax.rem(head, 2)
+    sibling = head + 1 - 2 * core
+    partner = lax.rem(head + 2, 4)
+    far = lax.rem(sibling + 2, 4)
+    source = (head, sibling, partner, far)
+    lat_cols, capacity = lat_t.shape[1], lat_t.shape[2]
+    span = capacity // CHUNKS
+
+    load_lat = pltpu.make_async_copy(lat_hbm, lat_v, load_sem.at[0])
+    load_vg = pltpu.make_async_copy(vg_hbm, vg_v, load_sem.at[1])
+    load_lat.start()
+    load_vg.start()
+
+    def peer(d):
+        return lax.rem(dp + d, n_dp)
+
+    barrier = pltpu.get_barrier_semaphore()
+    for h in (sibling, partner):
+        pl.semaphore_signal(barrier, inc=1, device_id=(dp, h), device_id_type=pl.DeviceIdType.MESH)
+    for d in range(1, n_dp):
+        pl.semaphore_signal(barrier, inc=1, device_id=(peer(d), head), device_id_type=pl.DeviceIdType.MESH)
+
+    load_lat.wait()
+    live = lax.broadcasted_iota(jnp.int32, (lat_cols, capacity), 1) < len_ref[dp]
+    turned = lat_v[...].T
+    lat_t[0] = jnp.where(live, turned, jnp.zeros_like(turned))
+    pl.semaphore_wait(barrier, n_dp + 1)
+
+    def remote(src, dst, ssem, rsem, where):
+        return pltpu.make_async_remote_copy(
+            src_ref=src, dst_ref=dst, send_sem=ssem, recv_sem=rsem,
+            device_id=where, device_id_type=pl.DeviceIdType.MESH,
+        )
+
+    def cut(k):
+        return pl.ds(k * span, span)
+
+    over = [
+        remote(lat_t.at[0, :, cut(k)], lat_t.at[2, :, cut(k)], x_send.at[k], x_recv.at[k], (dp, partner))
+        for k in range(CHUNKS)
+    ]
+    forward = [
+        remote(lat_t.at[2, :, cut(k)], lat_t.at[3, :, cut(k)], f_send.at[k], f_recv.at[k], (dp, sibling))
+        for k in range(CHUNKS)
+    ]
+    near = remote(lat_t.at[0], lat_t.at[1], sib_sem.at[0], sib_sem.at[1], (dp, sibling))
+    for c in over:
+        c.start()
+    near.start()
+
+    def scatter(s, d):
+        to = peer(d)
+        return remote(
+            part.at[s, pl.ds(pl.multiple_of(to * TILE, TILE), TILE)], rs_buf.at[s, d],
+            rs_send.at[s, d], rs_recv.at[s, d], (to, head),
+        )
+
+    def gather(s, d):
+        row = pl.multiple_of(source[s] * lat_cols + dp * TILE, TILE)
+        block = grad.at[pl.ds(row, TILE)]
+        return remote(block, block, ag_send.at[s, d], ag_recv.at[s, d], (peer(d), head))
+
+    def finish(s, total):
+        acc[s] = total
+        part[s] = total.astype(jnp.bfloat16)
+        for d in range(1, n_dp):
+            scatter(s, d).start()
+
+    def reduce(s):
+        total = acc[s, pl.ds(pl.multiple_of(dp * TILE, TILE), TILE), :]
+        for d in range(1, n_dp):
+            scatter(s, d).wait_recv()
+            total = total + rs_buf[s, d].astype(jnp.float32)
+        row = pl.multiple_of(source[s] * lat_cols + dp * TILE, TILE)
+        grad[pl.ds(row, TILE), :] = total.astype(jnp.bfloat16)
+        for d in range(1, n_dp):
+            gather(s, d).start()
+
+    def product(s, k=None):
+        if k is None:
+            return dot_f32(lat_t[s], vg_v[...], ((1,), (0,)))
+        return dot_f32(lat_t[s, :, cut(k)], vg_v[cut(k), :], ((1,), (0,)))
+
+    load_vg.wait()
+    finish(0, product(0))
+    near.wait_recv()
+    finish(1, product(1))
+
+    for k in range(CHUNKS):
+        over[k].wait_recv()
+        forward[k].start()
+        acc[2] = product(2, k) if k == 0 else acc[2] + product(2, k)
+        if k < 2:
+            reduce(k)
+    finish(2, acc[2])
+    for k in range(CHUNKS):
+        forward[k].wait_recv()
+        acc[3] = product(3, k) if k == 0 else acc[3] + product(3, k)
+    finish(3, acc[3])
+    reduce(2)
+    reduce(3)
+    for s in range(4):
+        for d in range(1, n_dp):
+            gather(s, d).wait_recv()
+
+    count = grad.shape[1] // V_DIM
+    done = newton_schulz([grad[:, pl.ds(h * V_DIM, V_DIM)] for h in range(count)])
+    for h in range(count):
+        out_ref[h] = done[h]
+
+    near.wait_send()
+    for k in range(CHUNKS):
+        over[k].wait_send()
+        forward[k].wait_send()
+    for s in range(4):
+        for d in range(1, n_dp):
+            scatter(s, d).wait_send()
+            gather(s, d).wait_send()
+
+
+def kernel_body(n_dp, latent, value_grad, lengths):
+    capacity, lat_cols = latent.shape
+    width = value_grad.shape[1]
+    dma = pltpu.SemaphoreType.DMA
+    return pl.pallas_call(
+        functools.partial(kernel, n_dp),
+        out_shape=jax.ShapeDtypeStruct((width // V_DIM, KV_RANK, V_DIM), jnp.bfloat16),
+        in_specs=[
+            pl.BlockSpec(memory_space=pltpu.SMEM),
+            pl.BlockSpec(memory_space=pl.ANY),
+            pl.BlockSpec(memory_space=pl.ANY),
+        ],
+        out_specs=pl.BlockSpec(memory_space=pltpu.VMEM),
+        scratch_shapes=[
+            pltpu.VMEM((capacity, lat_cols), jnp.bfloat16),
+            pltpu.VMEM((capacity, width), jnp.bfloat16),
+            pltpu.VMEM((4, lat_cols, capacity), jnp.bfloat16),
+            pltpu.VMEM((4, lat_cols, width), jnp.float32),
+            pltpu.VMEM((4, lat_cols, width), jnp.bfloat16),
+            pltpu.VMEM((4, n_dp, TILE, width), jnp.bfloat16),
+            pltpu.VMEM((KV_RANK, width), jnp.bfloat16),
+            dma((2,)), dma((2,)),
+            dma((CHUNKS,)), dma((CHUNKS,)), dma((CHUNKS,)), dma((CHUNKS,)),
+            dma((4, n_dp)), dma((4, n_dp)), dma((4, n_dp)), dma((4, n_dp)),
+        ],
+        compiler_params=pltpu.CompilerParams(
+            collective_id=0, has_side_effects=True, vmem_limit_bytes=40 * 2**20
+        ),
+        name="muon_update",
+    )(lengths, latent, value_grad)
+
+
 def solution(mesh):
+    n_dp, n_head = mesh.shape["dp"], mesh.shape["head"]
+    fits = n_head == 4 and (KV_RANK // n_head) == TILE * n_dp
+    body = functools.partial(kernel_body, n_dp) if fits else plain_body
     return jax.shard_map(
         body,
         mesh=mesh,

time: 164 us -> 41.3 us (0.25)
  waiting for transfers between devices: 86.9 us -> 0 us
  blocking collectives: 51.1 us -> 0 us
  Pallas kernels: 0 us -> 37.3 us
  between operations: 13.5 us -> 0.01 us
  matrix products: 7.7 us -> 0 us
    unnamed x3 -> x0, waiting for transfers between devices: 64.6 us -> none
    pallas_call x0 -> x1, Pallas kernels: none -> 37.3 us  [kernel_body(): pl.pallas_call(functools.partial(kernel, n_dp), out_shape=jax.ShapeDtypeS...]
    all_gather x1 -> x0, blocking collectives: 31.6 us -> none  [body(): ortho = lax.all_gather(ortho_shard, 'dp', axis=0, tiled=True)]
    all_gather x1 -> x0, waiting for transfers between devices: 22.3 us -> none  [body(): lax.all_gather(latent, 'head', axis=1, tiled=True)]
    psum x1 -> x0, blocking collectives: 19.5 us -> none  [body(): square_total = lax.psum(local_squares, 'dp')]
    dot_general x11 -> x0, matrix products: 7.7 us -> none  [the longest x1 2.99 us: body(): lax.dot_general(lax.all_gather(latent, 'head', axis=1, tiled=True), rows_...]
    unnamed x2 -> x7, local copies, waits for them, and re-layouts: 2.35 us -> 3.85 us
  transfers between devices with their start and end apart: 2 -> 0, of which waited for: 2 -> 0; matrix products, arithmetic and copies ran while one was open for 1% -> 0% of each run, Pallas kernels for 0% -> 0%
where the time goes in v1:
time: 41.3 us; the launch traced here: 41.2 us
  Pallas kernels  37.3 us (90%)
  local copies, waits for them, and re-layouts  3.85 us (9%)
    pallas_call x1, Pallas kernels, kernel_body(): pl.pallas_call(functools.partial(kernel, n_dp), out_shape=jax.ShapeDtypeS...  37.3 us
    unnamed x7, local copies, waits for them, and re-layouts  3.85 us

profile of v1, /device:TPU:0, one launch (start us, length us, event | category | flops | bytes accessed | tf_op | source)
XLA Modules:
  0.0 41.2 jit_solution(16963523227320502002)
XLA Ops:
  0.0 0.0 copy-start
  0.0 1.4 %copy-done = bf16[1536,512]{1,0:T(8,128)(2,1)S(1)} copy-done((bf16[1536,512]{1,0:T(8,128)(2,1)S(1)}, bf16[1536,512]{1,0:T(8,128)(2,1)}, u32[]{:S(2)}) %copy-start) | copy-done | bytes 1572888
  1.4 0.0 copy-start.1
  1.4 1.0 %copy-done.1 = bf16[1536,128]{1,0:T(8,128)(2,1)S(1)} copy-done((bf16[1536,128]{1,0:T(8,128)(2,1)S(1)}, bf16[1536,128]{1,0:T(8,128)(2,1)}, u32[]{:S(2)}) %copy-start.1) | copy-done | bytes 393240
  2.4 0.0 copy-start.2
  2.4 0.7 %copy-done.2 = s32[8]{0:T(128)S(1)} copy-done((s32[8]{0:T(128)S(1)}, s32[8]{0:T(128)}, u32[]{:S(2)}) %copy-start.2) | copy-done | bytes 56
  3.1 37.3 %muon_update.1 = bf16[4,512,128]{2,1,0:T(8,128)(2,1)S(1)} custom-call(s32[8]{0:T(128)S(1)} %copy-done.2, bf16[1536,128]{1,0:T(8,128)(2,1)S(1)} %copy-done.1, bf16[1536,512]{1,0:T(8,128)(2,1)S(1)} %copy-done), custom_call_target="tpu_custom_call" | custom-call | tf_op jit(solution)/shard_map/muon_update/pallas_call | solution.py:220
  40.4 0.8 %copy.5 = bf16[4,512,128]{2,1,0:T(8,128)(2,1)} copy(bf16[4,512,128]{2,1,0:T(8,128)(2,1)S(1)} %muon_update.1) | data formatting | bytes 1048576
Async XLA Ops:
  0.0 1.4 %copy-start = (bf16[1536,512]{1,0:T(8,128)(2,1)S(1)}, bf16[1536,512]{1,0:T(8,128)(2,1)}, u32[]{:S(2)}) copy-start(bf16[1536,512]{1,0:T(8,128)(2,1)} %vg_hbm.1) | copy-start | bytes 4718596
  1.4 1.0 %copy-start.1 = (bf16[1536,128]{1,0:T(8,128)(2,1)S(1)}, bf16[1536,128]{1,0:T(8,128)(2,1)}, u32[]{:S(2)}) copy-start(bf16[1536,128]{1,0:T(8,128)(2,1)} %lat_hbm.1) | copy-start | bytes 1179652
  2.4 0.7 %copy-start.2 = (s32[8]{0:T(128)S(1)}, s32[8]{0:T(128)}, u32[]{:S(2)}) copy-start(s32[8]{0:T(128)} %len_ref.1) | copy-start | bytes 100

commit v2 on v0

--- a/solution.py
+++ b/solution.py
@@ -1,12 +1,17 @@
+import functools
+
 import jax
 import jax.numpy as jnp
 from jax import lax
+from jax.experimental import pallas as pl
+from jax.experimental.pallas import tpu as pltpu
 from jax.sharding import PartitionSpec as P
 
 KV_RANK = 512
 V_DIM = 128
 ITERS = 5
-
+ROW_PARTS = 2
+TOKEN_PARTS = 2
 
 epsilon = 1e-07
 coef_one = 3.4445
@@ -14,7 +19,7 @@
 coef_three = 2.0315
 
 
-def body(latent, value_grad, lengths):
+def plain_body(latent, value_grad, lengths):
     capacity, lat_cols = latent.shape
     grad_width = value_grad.shape[1]
     head_count = grad_width // V_DIM
@@ -50,7 +55,291 @@
     return jnp.transpose(update, (1, 0, 2))
 
 
+def dot_f32(a, b, dims):
+    return lax.dot_general(a, b, (dims, ((), ())), preferred_element_type=jnp.float32)
+
+
+def newton_schulz(grads):
+    final = 0.2 * max(KV_RANK, V_DIM) ** 0.5
+    xs = list(grads)
+    inv = []
+    for g in xs:
+        w = g.astype(jnp.float32)
+        rows = jnp.sum(w * w, axis=0, keepdims=True)
+        inv.append(1.0 / (jnp.sqrt(jnp.sum(rows, axis=1, keepdims=True)) + epsilon))
+    for step in range(ITERS):
+        grams = [dot_f32(x, x, ((0,), (0,))) for x in xs]
+        if step == 0:
+            grams = [a * s * s for a, s in zip(grams, inv)]
+        grams = [a.astype(jnp.bfloat16) for a in grams]
+        squares = [dot_f32(a, a, ((1,), (0,))) for a in grams]
+        polys = [
+            (coef_two * a.astype(jnp.float32) + coef_three * q).astype(jnp.bfloat16)
+            for a, q in zip(grams, squares)
+        ]
+        prods = [dot_f32(x, b, ((1,), (0,))) for x, b in zip(xs, polys)]
+        wide = [coef_one * x.astype(jnp.float32) + p for x, p in zip(xs, prods)]
+        if step == 0:
+            wide = [x * s for x, s in zip(wide, inv)]
+        xs = [x.astype(jnp.bfloat16) for x in wide]
+    return [(final * x.astype(jnp.float32)).astype(jnp.bfloat16) for x in xs]
+
+
+def kernel(
+    depth,
+    len_hbm, lat_hbm, vg_hbm, out_ref,
+    len_s, lat_v, vg_v, lat_t, acc, part, ybuf, zacc, zpart, zbuf, grad,
+    load_sem, sib_sem, x_send, x_recv, f_send, f_recv,
+    y_send, y_recv, z_send, z_recv, a_send, a_recv, b_send, b_recv,
+):
+    dp = lax.axis_index("dp")
+    head = lax.axis_index("head")
+    y, z = lax.rem(dp, 2), lax.div(dp, 2)
+    core = lax.rem(head, 2)
+    sibling = head + 1 - 2 * core
+    partner = lax.rem(head + 2, 4)
+    far = lax.rem(sibling + 2, 4)
+    source = (head, sibling, partner, far)
+    across = dp + 1 - 2 * y
+    lat_cols, capacity = lat_t.shape[1], lat_t.shape[2]
+    half = acc.shape[3]
+    part_rows = lat_cols // ROW_PARTS
+    span = capacity // TOKEN_PARTS
+
+    def along(d):
+        return lax.rem(z + d, depth) * 2 + y
+
+    loads = [
+        pltpu.make_async_copy(src, dst, load_sem.at[i])
+        for i, (src, dst) in enumerate(((lat_hbm, lat_v), (len_hbm, len_s), (vg_hbm, vg_v)))
+    ]
+    for c in loads:
+        c.start()
+
+    barrier = pltpu.get_barrier_semaphore()
+    friends = [(dp, sibling), (dp, partner), (across, head)]
+    friends += [(along(d), head) for d in range(1, depth)]
+    for where in friends:
+        pl.semaphore_signal(barrier, inc=1, device_id=where, device_id_type=pl.DeviceIdType.MESH)
+
+    loads[0].wait()
+    loads[1].wait()
+    live = lax.broadcasted_iota(jnp.int32, (lat_cols, capacity), 1) < len_s[dp]
+    turned = lat_v[...].T
+    lat_t[0] = jnp.where(live, turned, jnp.zeros_like(turned))
+    pl.semaphore_wait(barrier, len(friends))
+
+    def remote(src, dst, ssem, rsem, where):
+        return pltpu.make_async_remote_copy(
+            src_ref=src, dst_ref=dst, send_sem=ssem, recv_sem=rsem,
+            device_id=where, device_id_type=pl.DeviceIdType.MESH,
+        )
+
+    pieces = [(c, k) for c in range(ROW_PARTS) for k in range(TOKEN_PARTS)]
+
+    def piece(slot, i):
+        c, k = pieces[i]
+        return lat_t.at[slot, pl.ds(c * part_rows, part_rows), pl.ds(k * span, span)]
+
+    over = [
+        remote(piece(0, i), piece(2, i), x_send.at[i], x_recv.at[i], (dp, partner))
+        for i in range(len(pieces))
+    ]
+    forward = [
+        remote(piece(2, i), piece(3, i), f_send.at[i], f_recv.at[i], (dp, sibling))
+        for i in range(len(pieces))
+    ]
+    near = remote(lat_t.at[0], lat_t.at[1], sib_sem.at[0], sib_sem.at[1], (dp, sibling))
+    over[0].start()
+    near.start()
+    for c in over[1:]:
+        c.start()
+
+    units = [(0, 0, lat_cols), (1, 0, lat_cols)]
+    units += [(s, c * part_rows, part_rows) for c in range(ROW_PARTS) for s in (2, 3)]
+
+    def spot(u, zz):
+        s, row, rows = units[u]
+        block = rows // depth
+        return pl.ds(pl.multiple_of(row + zz * block, block), block)
+
+    def grad_rows(u, zz=None):
+        s, row, rows = units[u]
+        if zz is None:
+            return pl.ds(pl.multiple_of(source[s] * lat_cols + row, rows), rows)
+        block = rows // depth
+        return pl.ds(pl.multiple_of(source[s] * lat_cols + row + zz * block, block), block)
+
+    def swap(u):
+        s, row, rows = units[u]
+        return remote(
+            part.at[s, 1 - y, pl.ds(row, rows)], ybuf.at[s, pl.ds(row, rows)],
+            y_send.at[u], y_recv.at[u], (across, head),
+        )
+
+    def scatter(u, d):
+        s, row, rows = units[u]
+        return remote(
+            zpart.at[s, spot(u, lax.rem(z + d, depth))],
+            zbuf.at[s, d, pl.ds(row // depth, rows // depth)],
+            z_send.at[u, d], z_recv.at[u, d], (along(d), head),
+        )
+
+    def gather(u, d):
+        block = grad.at[y, grad_rows(u, z)]
+        return remote(block, block, a_send.at[u, d], a_recv.at[u, d], (along(d), head))
+
+    def share(u):
+        block = grad.at[y, grad_rows(u)]
+        return remote(block, block, b_send.at[u], b_recv.at[u], (across, head))
+
+    def multiply(u, k=None):
+        s, row, rows = units[u]
+        tokens = pl.ds(0, capacity) if k is None else pl.ds(k * span, span)
+        lhs = lat_t[s, pl.ds(row, rows), tokens]
+        for j in range(2):
+            value = dot_f32(lhs, vg_v[tokens, pl.ds(j * half, half)], ((1,), (0,)))
+            if k:
+                value = value + acc[s, j, pl.ds(row, rows), :]
+            acc[s, j, pl.ds(row, rows), :] = value
+            if k is None or k == TOKEN_PARTS - 1:
+                part[s, j, pl.ds(row, rows), :] = value.astype(jnp.bfloat16)
+        if k is None or k == TOKEN_PARTS - 1:
+            swap(u).start()
+
+    def stage_z(u):
+        s, row, rows = units[u]
+        here = pl.ds(row, rows)
+        swap(u).wait_recv()
+        total = acc[s, y, here, :] + ybuf[s, here, :].astype(jnp.float32)
+        zacc[s, here, :] = total
+        zpart[s, here, :] = total.astype(jnp.bfloat16)
+        for d in range(1, depth):
+            scatter(u, d).start()
+
+    def stage_gather(u):
+        s, row, rows = units[u]
+        total = zacc[s, spot(u, z), :]
+        for d in range(1, depth):
+            scatter(u, d).wait_recv()
+            total = total + zbuf[s, d, pl.ds(row // depth, rows // depth), :].astype(jnp.float32)
+        grad[y, grad_rows(u, z), :] = total.astype(jnp.bfloat16)
+        for d in range(1, depth):
+            gather(u, d).start()
+
+    def stage_share(u):
+        for d in range(1, depth):
+            gather(u, d).wait_recv()
+        share(u).start()
+
+    def arrive(i):
+        over[i].wait_recv()
+        forward[i].start()
+
+    loads[2].wait()
+    multiply(0)
+    near.wait_recv()
+    multiply(1)
+    arrive(0)
+    multiply(2, 0)
+    stage_z(0)
+    arrive(1)
+    multiply(2, 1)
+    stage_z(1)
+    for i in (0, 1):
+        forward[i].wait_recv()
+        multiply(3, i)
+    stage_gather(0)
+    stage_gather(1)
+    arrive(2)
+    multiply(4, 0)
+    stage_z(2)
+    stage_share(0)
+    arrive(3)
+    multiply(4, 1)
+    stage_z(3)
+    for i in (2, 3):
+        forward[i].wait_recv()
+        multiply(5, i - 2)
+    stage_share(1)
+    stage_gather(2)
+    stage_gather(3)
+    stage_z(4)
+    stage_z(5)
+    stage_share(2)
+    stage_share(3)
+    stage_gather(4)
+    stage_gather(5)
+    stage_share(4)
+    stage_share(5)
+
+    count = half // V_DIM
+
+    def orthogonalize(side):
+        done = newton_schulz([grad[side, :, pl.ds(h * V_DIM, V_DIM)] for h in range(count)])
+        for h in range(count):
+            out_ref[side * count + h] = done[h]
+
+    orthogonalize(y)
+    for u in range(len(units)):
+        share(u).wait_recv()
+    orthogonalize(1 - y)
+
+    near.wait_send()
+    for i in range(len(pieces)):
+        over[i].wait_send()
+        forward[i].wait_send()
+    for u in range(len(units)):
+        swap(u).wait_send()
+        share(u).wait_send()
+        for d in range(1, depth):
+            scatter(u, d).wait_send()
+            gather(u, d).wait_send()
+
+
+def kernel_body(depth, latent, value_grad, lengths):
+    capacity, lat_cols = latent.shape
+    width = value_grad.shape[1]
+    half = width // 2
+    units, pieces = 2 + 2 * ROW_PARTS, ROW_PARTS * TOKEN_PARTS
+    dma = pltpu.SemaphoreType.DMA
+    low, full = jnp.bfloat16, jnp.float32
+    return pl.pallas_call(
+        functools.partial(kernel, depth),
+        out_shape=jax.ShapeDtypeStruct((width // V_DIM, KV_RANK, V_DIM), low),
+        in_specs=[pl.BlockSpec(memory_space=pltpu.HBM)] * 3,
+        out_specs=pl.BlockSpec(memory_space=pltpu.VMEM),
+        scratch_shapes=[
+            pltpu.SMEM(lengths.shape, jnp.int32),
+            pltpu.VMEM((capacity, lat_cols), low),
+            pltpu.VMEM((capacity, width), low),
+            pltpu.VMEM((4, lat_cols, capacity), low),
+            pltpu.VMEM((4, 2, lat_cols, half), full),
+            pltpu.VMEM((4, 2, lat_cols, half), low),
+            pltpu.VMEM((4, lat_cols, half), low),
+            pltpu.VMEM((4, lat_cols, half), full),
+            pltpu.VMEM((4, lat_cols, half), low),
+            pltpu.VMEM((4, depth, lat_cols // depth, half), low),
+            pltpu.VMEM((2, KV_RANK, half), low),
+            dma((3,)), dma((2,)),
+            dma((pieces,)), dma((pieces,)), dma((pieces,)), dma((pieces,)),
+            dma((units,)), dma((units,)),
+            dma((units, depth)), dma((units, depth)),
+            dma((units, depth)), dma((units, depth)),
+            dma((units,)), dma((units,)),
+        ],
+        compiler_params=pltpu.CompilerParams(
+            collective_id=0, has_side_effects=True, vmem_limit_bytes=48 * 2**20
+        ),
+        name="muon_update",
+    )(lengths, latent, value_grad)
+
+
 def solution(mesh):
+    n_dp, n_head = mesh.shape["dp"], mesh.shape["head"]
+    depth = n_dp // 2
+    fits = n_head == 4 and KV_RANK // n_head == 16 * ROW_PARTS * depth
+    body = functools.partial(kernel_body, depth) if fits else plain_body
     return jax.shard_map(
         body,
         mesh=mesh,

time: 164 us -> 42.1 us (0.26)
  waiting for transfers between devices: 86.9 us -> 0 us
  blocking collectives: 51.1 us -> 0 us
  Pallas kernels: 0 us -> 38 us
  between operations: 13.5 us -> 0.01 us
  matrix products: 7.7 us -> 0 us
    unnamed x3 -> x0, waiting for transfers between devices: 64.6 us -> none
    pallas_call x0 -> x1, Pallas kernels: none -> 38 us  [kernel_body(): pl.pallas_call(functools.partial(kernel, depth), out_shape=jax.ShapeDtype...]
    all_gather x1 -> x0, blocking collectives: 31.6 us -> none  [body(): ortho = lax.all_gather(ortho_shard, 'dp', axis=0, tiled=True)]
    all_gather x1 -> x0, waiting for transfers between devices: 22.3 us -> none  [body(): lax.all_gather(latent, 'head', axis=1, tiled=True)]
    psum x1 -> x0, blocking collectives: 19.5 us -> none  [body(): square_total = lax.psum(local_squares, 'dp')]
    dot_general x11 -> x0, matrix products: 7.7 us -> none  [the longest x1 2.99 us: body(): lax.dot_general(lax.all_gather(latent, 'head', axis=1, tiled=True), rows_...]
    unnamed x2 -> x7, local copies, waits for them, and re-layouts: 2.35 us -> 3.85 us
  transfers between devices with their start and end apart: 2 -> 0, of which waited for: 2 -> 0; matrix products, arithmetic and copies ran while one was open for 1% -> 0% of each run, Pallas kernels for 0% -> 0%
where the time goes in v2:
time: 42.1 us; the launch traced here: 41.9 us
  Pallas kernels  38 us (90%)
  local copies, waits for them, and re-layouts  3.85 us (9%)
    pallas_call x1, Pallas kernels, kernel_body(): pl.pallas_call(functools.partial(kernel, depth), out_shape=jax.ShapeDtype...  38 us
    unnamed x7, local copies, waits for them, and re-layouts  3.85 us

profile of v2, /device:TPU:0, one launch (start us, length us, event | category | flops | bytes accessed | tf_op | source)
XLA Modules:
  0.0 41.9 jit_solution(14091552637276408074)
XLA Ops:
  0.0 0.0 copy-start
  0.0 1.4 %copy-done = bf16[1536,512]{1,0:T(8,128)(2,1)S(1)} copy-done((bf16[1536,512]{1,0:T(8,128)(2,1)S(1)}, bf16[1536,512]{1,0:T(8,128)(2,1)}, u32[]{:S(2)}) %copy-start) | copy-done | bytes 1572888
  1.4 0.0 copy-start.1
  1.4 1.0 %copy-done.1 = bf16[1536,128]{1,0:T(8,128)(2,1)S(1)} copy-done((bf16[1536,128]{1,0:T(8,128)(2,1)S(1)}, bf16[1536,128]{1,0:T(8,128)(2,1)}, u32[]{:S(2)}) %copy-start.1) | copy-done | bytes 393240
  2.4 0.0 copy-start.2
  2.4 0.7 %copy-done.2 = s32[8]{0:T(128)S(1)} copy-done((s32[8]{0:T(128)S(1)}, s32[8]{0:T(128)}, u32[]{:S(2)}) %copy-start.2) | copy-done | bytes 56
  3.1 38.0 %muon_update.1 = bf16[4,512,128]{2,1,0:T(8,128)(2,1)S(1)} custom-call(s32[8]{0:T(128)S(1)} %copy-done.2, bf16[1536,128]{1,0:T(8,128)(2,1)S(1)} %copy-done.1, bf16[1536,512]{1,0:T(8,128)(2,1)S(1)} %copy-done), custom_call_target="tpu_custom_call" | custom-call | tf_op jit(solution)/shard_map/muon_update/pallas_call | solution.py:307
  41.1 0.8 %copy.5 = bf16[4,512,128]{2,1,0:T(8,128)(2,1)} copy(bf16[4,512,128]{2,1,0:T(8,128)(2,1)S(1)} %muon_update.1) | data formatting | bytes 1048576
Async XLA Ops:
  0.0 1.4 %copy-start = (bf16[1536,512]{1,0:T(8,128)(2,1)S(1)}, bf16[1536,512]{1,0:T(8,128)(2,1)}, u32[]{:S(2)}) copy-start(bf16[1536,512]{1,0:T(8,128)(2,1)} %vg_hbm.1) | copy-start | bytes 4718596
  1.4 1.0 %copy-start.1 = (bf16[1536,128]{1,0:T(8,128)(2,1)S(1)}, bf16[1536,128]{1,0:T(8,128)(2,1)}, u32[]{:S(2)}) copy-start(bf16[1536,128]{1,0:T(8,128)(2,1)} %lat_hbm.1) | copy-start | bytes 1179652
  2.4 0.7 %copy-start.2 = (s32[8]{0:T(128)S(1)}, s32[8]{0:T(128)}, u32[]{:S(2)}) copy-start(s32[8]{0:T(128)} %len_hbm.1) | copy-start | bytes 100

commit v3 on v2

--- a/solution.py
+++ b/solution.py
@@ -59,16 +59,16 @@
     return lax.dot_general(a, b, (dims, ((), ())), preferred_element_type=jnp.float32)
 
 
-def newton_schulz(grads):
+def newton_schulz(turned):
     final = 0.2 * max(KV_RANK, V_DIM) ** 0.5
-    xs = list(grads)
+    xs = list(turned)
     inv = []
     for g in xs:
         w = g.astype(jnp.float32)
         rows = jnp.sum(w * w, axis=0, keepdims=True)
         inv.append(1.0 / (jnp.sqrt(jnp.sum(rows, axis=1, keepdims=True)) + epsilon))
     for step in range(ITERS):
-        grams = [dot_f32(x, x, ((0,), (0,))) for x in xs]
+        grams = [dot_f32(x, x, ((1,), (1,))) for x in xs]
         if step == 0:
             grams = [a * s * s for a, s in zip(grams, inv)]
         grams = [a.astype(jnp.bfloat16) for a in grams]
@@ -77,19 +77,19 @@
             (coef_two * a.astype(jnp.float32) + coef_three * q).astype(jnp.bfloat16)
             for a, q in zip(grams, squares)
         ]
-        prods = [dot_f32(x, b, ((1,), (0,))) for x, b in zip(xs, polys)]
+        prods = [dot_f32(b, x, ((1,), (0,))) for x, b in zip(xs, polys)]
         wide = [coef_one * x.astype(jnp.float32) + p for x, p in zip(xs, prods)]
         if step == 0:
             wide = [x * s for x, s in zip(wide, inv)]
         xs = [x.astype(jnp.bfloat16) for x in wide]
-    return [(final * x.astype(jnp.float32)).astype(jnp.bfloat16) for x in xs]
+    return [(final * x.astype(jnp.float32)).astype(jnp.bfloat16).T for x in xs]
 
 
 def kernel(
     depth,
-    len_hbm, lat_hbm, vg_hbm, out_ref,
-    len_s, lat_v, vg_v, lat_t, acc, part, ybuf, zacc, zpart, zbuf, grad,
-    load_sem, sib_sem, x_send, x_recv, f_send, f_recv,
+    len_hbm, lat_hbm, vg_hbm, out_hbm,
+    len_s, lat_v, vg_v, lat_t, acc, part, ybuf, zacc, zpart, zbuf, grad, out_v,
+    load_sem, out_sem, sib_sem, x_send, x_recv, f_send, f_recv,
     y_send, y_recv, z_send, z_recv, a_send, a_recv, b_send, b_recv,
 ):
     dp = lax.axis_index("dp")
@@ -124,9 +124,14 @@
 
     loads[0].wait()
     loads[1].wait()
-    live = lax.broadcasted_iota(jnp.int32, (lat_cols, capacity), 1) < len_s[dp]
-    turned = lat_v[...].T
-    lat_t[0] = jnp.where(live, turned, jnp.zeros_like(turned))
+
+    def turn(k):
+        tokens = pl.ds(k * span, span)
+        turned = lat_v[tokens, :].T
+        live = lax.broadcasted_iota(jnp.int32, turned.shape, 1) + k * span < len_s[dp]
+        lat_t[0, :, tokens] = jnp.where(live, turned, jnp.zeros_like(turned))
+
+    turn(0)
     pl.semaphore_wait(barrier, len(friends))
 
     def remote(src, dst, ssem, rsem, where):
@@ -151,79 +156,76 @@
     ]
     near = remote(lat_t.at[0], lat_t.at[1], sib_sem.at[0], sib_sem.at[1], (dp, sibling))
     over[0].start()
+    for k in range(1, TOKEN_PARTS):
+        turn(k)
     near.start()
     for c in over[1:]:
         c.start()
 
-    units = [(0, 0, lat_cols), (1, 0, lat_cols)]
-    units += [(s, c * part_rows, part_rows) for c in range(ROW_PARTS) for s in (2, 3)]
-
-    def spot(u, zz):
+    units = [(0, 0, lat_cols)]
+    units += [(2, c * part_rows, part_rows) for c in range(ROW_PARTS)]
+
+    def rows_of(u):
+        s, row, rows = units[u]
+        return pl.ds(s, 2), pl.ds(row, rows)
+
+    def block_of(u, zz):
         s, row, rows = units[u]
         block = rows // depth
-        return pl.ds(pl.multiple_of(row + zz * block, block), block)
-
-    def grad_rows(u, zz=None):
+        return pl.ds(s, 2), pl.ds(pl.multiple_of(row + zz * block, block), block)
+
+    def buffer_of(u):
         s, row, rows = units[u]
-        if zz is None:
-            return pl.ds(pl.multiple_of(source[s] * lat_cols + row, rows), rows)
-        block = rows // depth
-        return pl.ds(pl.multiple_of(source[s] * lat_cols + row + zz * block, block), block)
+        return pl.ds(s, 2), pl.ds(row // depth, rows // depth)
 
     def swap(u):
-        s, row, rows = units[u]
+        slots, here = rows_of(u)
         return remote(
-            part.at[s, 1 - y, pl.ds(row, rows)], ybuf.at[s, pl.ds(row, rows)],
+            part.at[1 - y, slots, here], ybuf.at[slots, here],
             y_send.at[u], y_recv.at[u], (across, head),
         )
 
     def scatter(u, d):
-        s, row, rows = units[u]
         return remote(
-            zpart.at[s, spot(u, lax.rem(z + d, depth))],
-            zbuf.at[s, d, pl.ds(row // depth, rows // depth)],
+            zpart.at[block_of(u, lax.rem(z + d, depth))], zbuf.at[(d,) + buffer_of(u)],
             z_send.at[u, d], z_recv.at[u, d], (along(d), head),
         )
 
     def gather(u, d):
-        block = grad.at[y, grad_rows(u, z)]
+        block = grad.at[(y,) + block_of(u, z)]
         return remote(block, block, a_send.at[u, d], a_recv.at[u, d], (along(d), head))
 
     def share(u):
-        block = grad.at[y, grad_rows(u)]
+        block = grad.at[(y,) + rows_of(u)]
         return remote(block, block, b_send.at[u], b_recv.at[u], (across, head))
 
-    def multiply(u, k=None):
-        s, row, rows = units[u]
+    def multiply(s, row, rows, k=None):
         tokens = pl.ds(0, capacity) if k is None else pl.ds(k * span, span)
-        lhs = lat_t[s, pl.ds(row, rows), tokens]
+        here = pl.ds(row, rows)
+        lhs = lat_t[s, here, tokens]
         for j in range(2):
             value = dot_f32(lhs, vg_v[tokens, pl.ds(j * half, half)], ((1,), (0,)))
             if k:
-                value = value + acc[s, j, pl.ds(row, rows), :]
-            acc[s, j, pl.ds(row, rows), :] = value
+                value = value + acc[j, s, here, :]
+            acc[j, s, here, :] = value
             if k is None or k == TOKEN_PARTS - 1:
-                part[s, j, pl.ds(row, rows), :] = value.astype(jnp.bfloat16)
-        if k is None or k == TOKEN_PARTS - 1:
-            swap(u).start()
+                part[j, s, here, :] = value.astype(jnp.bfloat16)
 
     def stage_z(u):
-        s, row, rows = units[u]
-        here = pl.ds(row, rows)
+        here = rows_of(u)
         swap(u).wait_recv()
-        total = acc[s, y, here, :] + ybuf[s, here, :].astype(jnp.float32)
-        zacc[s, here, :] = total
-        zpart[s, here, :] = total.astype(jnp.bfloat16)
+        total = acc[(y,) + here] + ybuf[here].astype(jnp.float32)
+        zacc[here] = total
+        zpart[here] = total.astype(jnp.bfloat16)
         for d in range(1, depth):
             scatter(u, d).start()
 
     def stage_gather(u):
-        s, row, rows = units[u]
-        total = zacc[s, spot(u, z), :]
+        total = zacc[block_of(u, z)]
         for d in range(1, depth):
             scatter(u, d).wait_recv()
-            total = total + zbuf[s, d, pl.ds(row // depth, rows // depth), :].astype(jnp.float32)
-        grad[y, grad_rows(u, z), :] = total.astype(jnp.bfloat16)
+            total = total + zbuf[(d,) + buffer_of(u)].astype(jnp.float32)
+        grad[(y,) + block_of(u, z)] = total.astype(jnp.bfloat16)
         for d in range(1, depth):
             gather(u, d).start()
 
@@ -237,53 +239,53 @@
         forward[i].start()
 
     loads[2].wait()
-    multiply(0)
+    multiply(0, 0, lat_cols)
     near.wait_recv()
-    multiply(1)
-    arrive(0)
-    multiply(2, 0)
-    stage_z(0)
-    arrive(1)
-    multiply(2, 1)
-    stage_z(1)
-    for i in (0, 1):
-        forward[i].wait_recv()
-        multiply(3, i)
-    stage_gather(0)
+    multiply(1, 0, lat_cols)
+    swap(0).start()
+    for c in range(ROW_PARTS):
+        first = c * TOKEN_PARTS
+        for k in range(TOKEN_PARTS):
+            arrive(first + k)
+            multiply(2, c * part_rows, part_rows, k)
+            if c == 0 and k == 0:
+                stage_z(0)
+            if c == 1 and k == 0:
+                stage_z(1)
+        if c == 0:
+            stage_gather(0)
+        for k in range(TOKEN_PARTS):
+            forward[first + k].wait_recv()
+            multiply(3, c * part_rows, part_rows, k)
+        swap(1 + c).start()
+    stage_share(0)
     stage_gather(1)
-    arrive(2)
-    multiply(4, 0)
     stage_z(2)
-    stage_share(0)
-    arrive(3)
-    multiply(4, 1)
-    stage_z(3)
-    for i in (2, 3):
-        forward[i].wait_recv()
-        multiply(5, i - 2)
     stage_share(1)
     stage_gather(2)
-    stage_gather(3)
-    stage_z(4)
-    stage_z(5)
     stage_share(2)
-    stage_share(3)
-    stage_gather(4)
-    stage_gather(5)
-    stage_share(4)
-    stage_share(5)
 
     count = half // V_DIM
 
     def orthogonalize(side):
-        done = newton_schulz([grad[side, :, pl.ds(h * V_DIM, V_DIM)] for h in range(count)])
+        whole = grad[side].reshape(4 * lat_cols, half).T
+        done = newton_schulz([whole[h * V_DIM : (h + 1) * V_DIM] for h in range(count)])
         for h in range(count):
-            out_ref[side * count + h] = done[h]
+            for s in range(4):
+                row = pl.multiple_of(source[s] * lat_cols, lat_cols)
+                out_v[side, h, pl.ds(row, lat_cols), :] = done[h][s * lat_cols : (s + 1) * lat_cols]
+
+    def store(i, side):
+        return pltpu.make_async_copy(
+            out_v.at[side], out_hbm.at[pl.ds(side * count, count)], out_sem.at[i]
+        )
 
     orthogonalize(y)
+    store(0, y).start()
     for u in range(len(units)):
         share(u).wait_recv()
     orthogonalize(1 - y)
+    store(1, 1 - y).start()
 
     near.wait_send()
     for i in range(len(pieces)):
@@ -295,33 +297,36 @@
         for d in range(1, depth):
             scatter(u, d).wait_send()
             gather(u, d).wait_send()
+    store(0, y).wait()
+    store(1, 1 - y).wait()
 
 
 def kernel_body(depth, latent, value_grad, lengths):
     capacity, lat_cols = latent.shape
     width = value_grad.shape[1]
     half = width // 2
-    units, pieces = 2 + 2 * ROW_PARTS, ROW_PARTS * TOKEN_PARTS
+    units, pieces = 1 + ROW_PARTS, ROW_PARTS * TOKEN_PARTS
     dma = pltpu.SemaphoreType.DMA
     low, full = jnp.bfloat16, jnp.float32
     return pl.pallas_call(
         functools.partial(kernel, depth),
         out_shape=jax.ShapeDtypeStruct((width // V_DIM, KV_RANK, V_DIM), low),
         in_specs=[pl.BlockSpec(memory_space=pltpu.HBM)] * 3,
-        out_specs=pl.BlockSpec(memory_space=pltpu.VMEM),
+        out_specs=pl.BlockSpec(memory_space=pltpu.HBM),
         scratch_shapes=[
             pltpu.SMEM(lengths.shape, jnp.int32),
             pltpu.VMEM((capacity, lat_cols), low),
             pltpu.VMEM((capacity, width), low),
             pltpu.VMEM((4, lat_cols, capacity), low),
-            pltpu.VMEM((4, 2, lat_cols, half), full),
-            pltpu.VMEM((4, 2, lat_cols, half), low),
+            pltpu.VMEM((2, 4, lat_cols, half), full),
+            pltpu.VMEM((2, 4, lat_cols, half), low),
             pltpu.VMEM((4, lat_cols, half), low),
             pltpu.VMEM((4, lat_cols, half), full),
             pltpu.VMEM((4, lat_cols, half), low),
-            pltpu.VMEM((4, depth, lat_cols // depth, half), low),
-            pltpu.VMEM((2, KV_RANK, half), low),
-            dma((3,)), dma((2,)),
+            pltpu.VMEM((depth, 4, lat_cols // depth, half), low),
+            pltpu.VMEM((2, 4, lat_cols, half), low),
+            pltpu.VMEM((2, half // V_DIM, KV_RANK, V_DIM), low),
+            dma((3,)), dma((2,)), dma((2,)),
             dma((pieces,)), dma((pieces,)), dma((pieces,)), dma((pieces,)),
             dma((units,)), dma((units,)),
             dma((units, depth)), dma((units, depth)),
@@ -329,7 +334,7 @@
             dma((units,)), dma((units,)),
         ],
         compiler_params=pltpu.CompilerParams(
-            collective_id=0, has_side_effects=True, vmem_limit_bytes=48 * 2**20
+            collective_id=0, has_side_effects=True, vmem_limit_bytes=63 * 2**20
         ),
         name="muon_update",
     )(lengths, latent, value_grad)

time: 42.1 us -> 42 us (level)
  local copies, waits for them, and re-layouts: 3.85 us -> 1.87 us
  Pallas kernels: 38 us -> 39.9 us
    unnamed x7 -> x1, local copies, waits for them, and re-layouts: 3.85 us -> 1.87 us
    pallas_call x1, Pallas kernels: 38 us -> 39.9 us  [kernel_body(): pl.pallas_call(functools.partial(kernel, depth), out_shape=jax.ShapeDtype...]
where the time goes in v3:
time: 42 us; the launch traced here: 41.8 us
  Pallas kernels  39.9 us (95%)
  local copies, waits for them, and re-layouts  1.87 us (4%)
    pallas_call x1, Pallas kernels, kernel_body(): pl.pallas_call(functools.partial(kernel, depth), out_shape=jax.ShapeDtype...  39.9 us
    unnamed x1, local copies, waits for them, and re-layouts  1.87 us

profile of v3, /device:TPU:0, one launch (start us, length us, event | category | flops | bytes accessed | tf_op | source)
XLA Modules:
  0.0 41.8 jit_solution(6198447721557350622)
XLA Ops:
  0.0 39.9 %muon_update.1 = bf16[4,512,128]{2,1,0:T(8,128)(2,1)} custom-call(s32[8]{0:T(128)} %len_hbm.1, bf16[1536,128]{1,0:T(8,128)(2,1)} %lat_hbm.1, bf16[1536,512]{1,0:T(8,128)(2,1)} %vg_hbm.1), custom_call_target="tpu_custom_call" | custom-call | tf_op jit(solution)/shard_map/muon_update/pallas_call | solution.py:311
  40.0 1.9 %copy.5 = bf16[4,512,128]{2,1,0:T(8,128)(2,1)} copy(bf16[4,512,128]{2,1,0:T(8,128)(2,1)} %muon_update.1) | data formatting | bytes 1048576

commit v4 on v3

--- a/solution.py
+++ b/solution.py
@@ -59,37 +59,31 @@
     return lax.dot_general(a, b, (dims, ((), ())), preferred_element_type=jnp.float32)
 
 
-def newton_schulz(turned):
-    final = 0.2 * max(KV_RANK, V_DIM) ** 0.5
-    xs = list(turned)
-    inv = []
-    for g in xs:
-        w = g.astype(jnp.float32)
-        rows = jnp.sum(w * w, axis=0, keepdims=True)
-        inv.append(1.0 / (jnp.sqrt(jnp.sum(rows, axis=1, keepdims=True)) + epsilon))
+def newton_schulz(grads):
+    wide = grads.astype(jnp.float32)
+    inv = 1.0 / (jnp.sqrt(jnp.sum(wide * wide, axis=(1, 2), keepdims=True)) + epsilon)
+    ortho = grads
     for step in range(ITERS):
-        grams = [dot_f32(x, x, ((1,), (1,))) for x in xs]
+        gram = jnp.einsum("hrv,hrw->hvw", ortho, ortho, preferred_element_type=jnp.float32)
         if step == 0:
-            grams = [a * s * s for a, s in zip(grams, inv)]
-        grams = [a.astype(jnp.bfloat16) for a in grams]
-        squares = [dot_f32(a, a, ((1,), (0,))) for a in grams]
-        polys = [
-            (coef_two * a.astype(jnp.float32) + coef_three * q).astype(jnp.bfloat16)
-            for a, q in zip(grams, squares)
-        ]
-        prods = [dot_f32(b, x, ((1,), (0,))) for x, b in zip(xs, polys)]
-        wide = [coef_one * x.astype(jnp.float32) + p for x, p in zip(xs, prods)]
+            gram = gram * inv * inv
+        gram = gram.astype(jnp.bfloat16)
+        squared = jnp.einsum("hvu,huw->hvw", gram, gram, preferred_element_type=jnp.float32)
+        poly = (coef_two * gram.astype(jnp.float32) + coef_three * squared).astype(jnp.bfloat16)
+        product = jnp.einsum("hrv,hvw->hrw", ortho, poly, preferred_element_type=jnp.float32)
+        wide = coef_one * ortho.astype(jnp.float32) + product
         if step == 0:
-            wide = [x * s for x, s in zip(wide, inv)]
-        xs = [x.astype(jnp.bfloat16) for x in wide]
-    return [(final * x.astype(jnp.float32)).astype(jnp.bfloat16).T for x in xs]
+            wide = wide * inv
+        ortho = wide.astype(jnp.bfloat16)
+    scale = 0.2 * max(KV_RANK, V_DIM) ** 0.5
+    return (scale * ortho.astype(jnp.float32)).astype(jnp.bfloat16)
 
 
 def kernel(
     depth,
-    len_hbm, lat_hbm, vg_hbm, out_hbm,
-    len_s, lat_v, vg_v, lat_t, acc, part, ybuf, zacc, zpart, zbuf, grad, out_v,
-    load_sem, out_sem, sib_sem, x_send, x_recv, f_send, f_recv,
+    len_hbm, lat_hbm, vg_hbm, grad,
+    len_s, lat_v, vg_v, lat_t, acc, part, ybuf, zacc, zpart, zbuf,
+    load_sem, sib_sem, x_send, x_recv, f_send, f_recv,
     y_send, y_recv, z_send, z_recv, a_send, a_recv, b_send, b_recv,
 ):
     dp = lax.axis_index("dp")
@@ -103,6 +97,7 @@
     across = dp + 1 - 2 * y
     lat_cols, capacity = lat_t.shape[1], lat_t.shape[2]
     half = acc.shape[3]
+    count = half // V_DIM
     part_rows = lat_cols // ROW_PARTS
     span = capacity // TOKEN_PARTS
 
@@ -162,8 +157,9 @@
     for c in over[1:]:
         c.start()
 
-    units = [(0, 0, lat_cols)]
-    units += [(2, c * part_rows, part_rows) for c in range(ROW_PARTS)]
+    own, other = head - core, partner - core
+    units = [(own, 0, lat_cols)]
+    units += [(other, c * part_rows, part_rows) for c in range(ROW_PARTS)]
 
     def rows_of(u):
         s, row, rows = units[u]
@@ -192,11 +188,11 @@
         )
 
     def gather(u, d):
-        block = grad.at[(y,) + block_of(u, z)]
+        block = grad.at[(pl.ds(y * count, count),) + block_of(u, z)]
         return remote(block, block, a_send.at[u, d], a_recv.at[u, d], (along(d), head))
 
     def share(u):
-        block = grad.at[(y,) + rows_of(u)]
+        block = grad.at[(pl.ds(y * count, count),) + rows_of(u)]
         return remote(block, block, b_send.at[u], b_recv.at[u], (across, head))
 
     def multiply(s, row, rows, k=None):
@@ -206,10 +202,10 @@
         for j in range(2):
             value = dot_f32(lhs, vg_v[tokens, pl.ds(j * half, half)], ((1,), (0,)))
             if k:
-                value = value + acc[j, s, here, :]
-            acc[j, s, here, :] = value
+                value = value + acc[j, source[s], here, :]
+            acc[j, source[s], here, :] = value
             if k is None or k == TOKEN_PARTS - 1:
-                part[j, s, here, :] = value.astype(jnp.bfloat16)
+                part[j, source[s], here, :] = value.astype(jnp.bfloat16)
 
     def stage_z(u):
         here = rows_of(u)
@@ -225,7 +221,9 @@
         for d in range(1, depth):
             scatter(u, d).wait_recv()
             total = total + zbuf[(d,) + buffer_of(u)].astype(jnp.float32)
-        grad[(y,) + block_of(u, z)] = total.astype(jnp.bfloat16)
+        for h in range(count):
+            columns = total[..., h * V_DIM : (h + 1) * V_DIM]
+            grad[(y * count + h,) + block_of(u, z)] = columns.astype(jnp.bfloat16)
         for d in range(1, depth):
             gather(u, d).start()
 
@@ -265,27 +263,8 @@
     stage_gather(2)
     stage_share(2)
 
-    count = half // V_DIM
-
-    def orthogonalize(side):
-        whole = grad[side].reshape(4 * lat_cols, half).T
-        done = newton_schulz([whole[h * V_DIM : (h + 1) * V_DIM] for h in range(count)])
-        for h in range(count):
-            for s in range(4):
-                row = pl.multiple_of(source[s] * lat_cols, lat_cols)
-                out_v[side, h, pl.ds(row, lat_cols), :] = done[h][s * lat_cols : (s + 1) * lat_cols]
-
-    def store(i, side):
-        return pltpu.make_async_copy(
-            out_v.at[side], out_hbm.at[pl.ds(side * count, count)], out_sem.at[i]
-        )
-
-    orthogonalize(y)
-    store(0, y).start()
     for u in range(len(units)):
         share(u).wait_recv()
-    orthogonalize(1 - y)
-    store(1, 1 - y).start()
 
     near.wait_send()
     for i in range(len(pieces)):
@@ -297,8 +276,6 @@
         for d in range(1, depth):
             scatter(u, d).wait_send()
             gather(u, d).wait_send()
-    store(0, y).wait()
-    store(1, 1 - y).wait()
 
 
 def kernel_body(depth, latent, value_grad, lengths):
@@ -308,11 +285,14 @@
     units, pieces = 1 + ROW_PARTS, ROW_PARTS * TOKEN_PARTS
     dma = pltpu.SemaphoreType.DMA
     low, full = jnp.bfloat16, jnp.float32
-    return pl.pallas_call(
+    latent, value_grad, lengths = (
+        pltpu.with_memory_space_constraint(a, pltpu.HBM) for a in (latent, value_grad, lengths)
+    )
+    sums = pl.pallas_call(
         functools.partial(kernel, depth),
-        out_shape=jax.ShapeDtypeStruct((width // V_DIM, KV_RANK, V_DIM), low),
+        out_shape=pltpu.VMEM((width // V_DIM, 4, lat_cols, V_DIM), low),
         in_specs=[pl.BlockSpec(memory_space=pltpu.HBM)] * 3,
-        out_specs=pl.BlockSpec(memory_space=pltpu.HBM),
+        out_specs=pl.BlockSpec(memory_space=pltpu.VMEM),
         scratch_shapes=[
             pltpu.SMEM(lengths.shape, jnp.int32),
             pltpu.VMEM((capacity, lat_cols), low),
@@ -324,9 +304,7 @@
             pltpu.VMEM((4, lat_cols, half), full),
             pltpu.VMEM((4, lat_cols, half), low),
             pltpu.VMEM((depth, 4, lat_cols // depth, half), low),
-            pltpu.VMEM((2, 4, lat_cols, half), low),
-            pltpu.VMEM((2, half // V_DIM, KV_RANK, V_DIM), low),
-            dma((3,)), dma((2,)), dma((2,)),
+            dma((3,)), dma((2,)),
             dma((pieces,)), dma((pieces,)), dma((pieces,)), dma((pieces,)),
             dma((units,)), dma((units,)),
             dma((units, depth)), dma((units, depth)),
@@ -334,10 +312,11 @@
             dma((units,)), dma((units,)),
         ],
         compiler_params=pltpu.CompilerParams(
-            collective_id=0, has_side_effects=True, vmem_limit_bytes=63 * 2**20
+            collective_id=0, has_side_effects=True, vmem_limit_bytes=48 * 2**20
         ),
-        name="muon_update",
+        name="gradient_sums",
     )(lengths, latent, value_grad)
+    return newton_schulz(sums.reshape(width // V_DIM, KV_RANK, V_DIM))
 
 
 def solution(mesh):

time: 42 us -> 41.9 us (level)
  matrix products: 0 us -> 4.8 us
  Pallas kernels: 39.9 us -> 36.7 us
  local copies, waits for them, and re-layouts: 1.87 us -> 0 us
    dot_general x0 -> x10, matrix products: none -> 4.8 us  [the longest x5 2.98 us: newton_schulz(): jnp.einsum('hrv,hvw->hrw', ortho, poly, preferred_element_type=jnp.float32)]
    pallas_call x1, Pallas kernels: 39.9 us -> 36.7 us  [kernel_body(): pl.pallas_call(functools.partial(kernel, depth), out_shape=pltpu.VMEM((wi...]
    unnamed x1 -> x0, local copies, waits for them, and re-layouts: 1.87 us -> none
where the time goes in v4:
time: 41.9 us; the launch traced here: 41.8 us
  Pallas kernels  36.7 us (88%)
  matrix products  4.8 us (11%)
    pallas_call x1, Pallas kernels, kernel_body(): pl.pallas_call(functools.partial(kernel, depth), out_shape=pltpu.VMEM((wi...  36.7 us
    dot_general x5, matrix products, newton_schulz(): jnp.einsum('hrv,hvw->hrw', ortho, poly, preferred_element_type=jnp.float32)  2.98 us
    dot_general x5, matrix products, newton_schulz(): jnp.einsum('hrv,hrw->hvw', ortho, ortho, preferred_element_type=jnp.float32)  1.82 us

profile of v4, /device:TPU:0, one launch (start us, length us, event | category | flops | bytes accessed | tf_op | source)
XLA Modules:
  0.0 41.8 jit_solution(6669972443531339554)
XLA Ops:
  0.0 36.7 %gradient_sums.1 = bf16[4,4,128,128]{3,2,1,0:T(8,128)(2,1)S(1)} custom-call(s32[8]{0:T(128)} %len_hbm.1, bf16[1536,128]{1,0:T(8,128)(2,1)} %lat_hbm.1, bf16[1536,512]{1,0:T(8,128)(2,1)} %vg_hbm.1), custom_call_target="tpu_custom_call" | custom-call | tf_op jit(solution)/shard_map/gradient_sums/pallas_call | solution.py:291
  36.7 0.2 multiply_reduce_fusion
  36.9 0.4 %fusion.20 = bf16[4,128,128]{2,1,0:T(8,128)(2,1)S(1)} fusion(bf16[4,512,128]{2,1,0:T(8,128)(2,1)S(1)} %bitcast.26, f32[4]{0:T(128)S(1)} %add_divide_fusion), kind=kOutput, calls=%fused_computation.35 | convolution fusion | flops 67305472 | bytes 655376 | tf_op jit(solution)/shard_map/hrv,hrw->hvw/dot_general | solution.py:67
  37.3 0.4 %fusion.1 = bf16[4,512,128]{2,1,0:T(8,128)(2,1)S(1)} fusion(bf16[4,512,128]{2,1,0:T(8,128)(2,1)S(1)} %bitcast.27, bf16[4,128,128]{2,1,0:T(8,128)(2,1)S(1)} %fusion.20, f32[4]{0:T(128)S(1)} %add_divide_fusion), kind=kOutput, calls=%fused_computation.6 | convolution fusion | flops 85524480 | bytes 1179664 | tf_op jit(solution)/shard_map/hrv,hvw->hrw/dot_general | solution.py:73
  37.8 0.4 convolution_convert_fusion.3
  38.1 0.4 %fusion.2 = bf16[4,512,128]{2,1,0:T(8,128)(2,1)S(1)} fusion(bf16[4,512,128]{2,1,0:T(8,128)(2,1)S(1)} %fusion.1, bf16[4,128,128]{2,1,0:T(8,128)(2,1)S(1)} %convolution_convert_fusion.3), kind=kOutput, calls=%fused_computation.7 | convolution fusion | flops 85262336 | bytes 1179648 | tf_op jit(solution)/shard_map/hrv,hvw->hrw/dot_general | solution.py:73
  38.6 0.3 convolution_convert_fusion.2
  38.9 0.4 %fusion.3 = bf16[4,512,128]{2,1,0:T(8,128)(2,1)S(1)} fusion(bf16[4,512,128]{2,1,0:T(8,128)(2,1)S(1)} %fusion.2, bf16[4,128,128]{2,1,0:T(8,128)(2,1)S(1)} %convolution_convert_fusion.2), kind=kOutput, calls=%fused_computation.8 | convolution fusion | flops 85262336 | bytes 1179648 | tf_op jit(solution)/shard_map/hrv,hvw->hrw/dot_general | solution.py:73
  39.4 0.3 convolution_convert_fusion.1
  39.7 0.4 %fusion.4 = bf16[4,512,128]{2,1,0:T(8,128)(2,1)S(1)} fusion(bf16[4,512,128]{2,1,0:T(8,128)(2,1)S(1)} %fusion.3, bf16[4,128,128]{2,1,0:T(8,128)(2,1)S(1)} %convolution_convert_fusion.1), kind=kOutput, calls=%fused_computation.9 | convolution fusion | flops 85262336 | bytes 1179648 | tf_op jit(solution)/shard_map/hrv,hvw->hrw/dot_general | solution.py:73
  40.2 0.3 convolution_convert_fusion
  40.5 1.2 %fusion.8 = bf16[4,512,128]{2,1,0:T(8,128)(2,1)} fusion(bf16[4,512,128]{2,1,0:T(8,128)(2,1)S(1)} %fusion.4, bf16[4,128,128]{2,1,0:T(8,128)(2,1)S(1)} %convolution_convert_fusion), kind=kOutput, calls=%fused_computation.13 | convolution fusion | flops 86048768 | bytes 1179648 | tf_op jit(solution)/shard_map/hrv,hvw->hrw/dot_general | solution.py:73
  (1 shorter events, 0.0 us)

commit v5 on v4

--- a/solution.py
+++ b/solution.py
@@ -11,7 +11,7 @@
 V_DIM = 128
 ITERS = 5
 ROW_PARTS = 2
-TOKEN_PARTS = 2
+TOKEN_PARTS = 3
 
 epsilon = 1e-07
 coef_one = 3.4445
@@ -82,9 +82,10 @@
 def kernel(
     depth,
     len_hbm, lat_hbm, vg_hbm, grad,
-    len_s, lat_v, vg_v, lat_t, acc, part, ybuf, zacc, zpart, zbuf,
+    len_s, lat_v, vg_v, lat_t, acc, part, ybuf, zacc, zpart, zbuf, dbuf,
     load_sem, sib_sem, x_send, x_recv, f_send, f_recv,
     y_send, y_recv, z_send, z_recv, a_send, a_recv, b_send, b_recv,
+    d_send, d_recv, e_send, e_recv,
 ):
     dp = lax.axis_index("dp")
     head = lax.axis_index("head")
@@ -104,6 +105,12 @@
     def along(d):
         return lax.rem(z + d, depth) * 2 + y
 
+    def side(far_y):
+        return 1 - y if far_y else y
+
+    def other_dp(far_y, d):
+        return lax.rem(z + d, depth) * 2 + side(far_y)
+
     loads = [
         pltpu.make_async_copy(src, dst, load_sem.at[i])
         for i, (src, dst) in enumerate(((lat_hbm, lat_v), (len_hbm, len_s), (vg_hbm, vg_v)))
@@ -112,8 +119,9 @@
         c.start()
 
     barrier = pltpu.get_barrier_semaphore()
-    friends = [(dp, sibling), (dp, partner), (across, head)]
-    friends += [(along(d), head) for d in range(1, depth)]
+    others = [(far_y, d) for far_y in range(2) for d in range(depth) if far_y or d]
+    friends = [(dp, sibling), (dp, partner)]
+    friends += [(other_dp(*o), head) for o in others]
     for where in friends:
         pl.semaphore_signal(barrier, inc=1, device_id=where, device_id_type=pl.DeviceIdType.MESH)
 
@@ -195,17 +203,31 @@
         block = grad.at[(pl.ds(y * count, count),) + rows_of(u)]
         return remote(block, block, b_send.at[u], b_recv.at[u], (across, head))
 
+    def scatter_all(u, far_y, d):
+        i = far_y * depth + d
+        return remote(
+            part.at[(side(far_y),) + block_of(u, lax.rem(z + d, depth))], dbuf.at[i],
+            d_send.at[i], d_recv.at[i], (other_dp(far_y, d), head),
+        )
+
+    def gather_all(u, far_y, d):
+        i = far_y * depth + d
+        block = grad.at[(pl.ds(y * count, count),) + block_of(u, z)]
+        return remote(block, block, e_send.at[i], e_recv.at[i], (other_dp(far_y, d), head))
+
     def multiply(s, row, rows, k=None):
         tokens = pl.ds(0, capacity) if k is None else pl.ds(k * span, span)
         here = pl.ds(row, rows)
-        lhs = lat_t[s, here, tokens]
+        lhs = jnp.concatenate([lat_t[i, here, tokens] for i in s], axis=0)
         for j in range(2):
             value = dot_f32(lhs, vg_v[tokens, pl.ds(j * half, half)], ((1,), (0,)))
-            if k:
-                value = value + acc[j, source[s], here, :]
-            acc[j, source[s], here, :] = value
-            if k is None or k == TOKEN_PARTS - 1:
-                part[j, source[s], here, :] = value.astype(jnp.bfloat16)
+            for n, i in enumerate(s):
+                mine = value[n * rows : (n + 1) * rows]
+                if k:
+                    mine = mine + acc[j, source[i], here, :]
+                acc[j, source[i], here, :] = mine
+                if k is None or k == TOKEN_PARTS - 1:
+                    part[j, source[i], here, :] = mine.astype(jnp.bfloat16)
 
     def stage_z(u):
         here = rows_of(u)
@@ -221,11 +243,23 @@
         for d in range(1, depth):
             scatter(u, d).wait_recv()
             total = total + zbuf[(d,) + buffer_of(u)].astype(jnp.float32)
+        keep(u, total)
+        for d in range(1, depth):
+            gather(u, d).start()
+
+    def keep(u, total):
         for h in range(count):
             columns = total[..., h * V_DIM : (h + 1) * V_DIM]
             grad[(y * count + h,) + block_of(u, z)] = columns.astype(jnp.bfloat16)
-        for d in range(1, depth):
-            gather(u, d).start()
+
+    def reduce_all(u):
+        total = acc[(y,) + block_of(u, z)]
+        for o in others:
+            scatter_all(u, *o).wait_recv()
+            total = total + dbuf[o[0] * depth + o[1]].astype(jnp.float32)
+        keep(u, total)
+        for o in others:
+            gather_all(u, *o).start()
 
     def stage_share(u):
         for d in range(1, depth):
@@ -236,41 +270,43 @@
         over[i].wait_recv()
         forward[i].start()
 
+    last = len(units) - 1
     loads[2].wait()
-    multiply(0, 0, lat_cols)
+    multiply([0], 0, lat_cols)
     near.wait_recv()
-    multiply(1, 0, lat_cols)
+    multiply([1], 0, lat_cols)
     swap(0).start()
     for c in range(ROW_PARTS):
-        first = c * TOKEN_PARTS
         for k in range(TOKEN_PARTS):
-            arrive(first + k)
-            multiply(2, c * part_rows, part_rows, k)
-            if c == 0 and k == 0:
-                stage_z(0)
-            if c == 1 and k == 0:
-                stage_z(1)
+            i = c * TOKEN_PARTS + k
+            arrive(i)
+            if k == 1:
+                stage_z(c)
+            if c == 1 and k == 2:
+                stage_gather(1)
+            forward[i].wait_recv()
+            multiply([2, 3], c * part_rows, part_rows, k)
         if c == 0:
+            swap(1).start()
             stage_gather(0)
-        for k in range(TOKEN_PARTS):
-            forward[first + k].wait_recv()
-            multiply(3, c * part_rows, part_rows, k)
-        swap(1 + c).start()
+    for o in others:
+        scatter_all(last, *o).start()
     stage_share(0)
-    stage_gather(1)
-    stage_z(2)
+    reduce_all(last)
     stage_share(1)
-    stage_gather(2)
-    stage_share(2)
-
-    for u in range(len(units)):
+    for u in range(last):
         share(u).wait_recv()
+    for o in others:
+        gather_all(last, *o).wait_recv()
 
     near.wait_send()
     for i in range(len(pieces)):
         over[i].wait_send()
         forward[i].wait_send()
-    for u in range(len(units)):
+    for o in others:
+        scatter_all(last, *o).wait_send()
+        gather_all(last, *o).wait_send()
+    for u in range(last):
         swap(u).wait_send()
         share(u).wait_send()
         for d in range(1, depth):
@@ -282,7 +318,7 @@
     capacity, lat_cols = latent.shape
     width = value_grad.shape[1]
     half = width // 2
-    units, pieces = 1 + ROW_PARTS, ROW_PARTS * TOKEN_PARTS
+    units, pieces = ROW_PARTS, ROW_PARTS * TOKEN_PARTS
     dma = pltpu.SemaphoreType.DMA
     low, full = jnp.bfloat16, jnp.float32
     latent, value_grad, lengths = (
@@ -304,12 +340,14 @@
             pltpu.VMEM((4, lat_cols, half), full),
             pltpu.VMEM((4, lat_cols, half), low),
             pltpu.VMEM((depth, 4, lat_cols // depth, half), low),
+            pltpu.VMEM((2 * depth, 2, lat_cols // ROW_PARTS // depth, half), low),
             dma((3,)), dma((2,)),
             dma((pieces,)), dma((pieces,)), dma((pieces,)), dma((pieces,)),
             dma((units,)), dma((units,)),
             dma((units, depth)), dma((units, depth)),
             dma((units, depth)), dma((units, depth)),
             dma((units,)), dma((units,)),
+            dma((2 * depth,)), dma((2 * depth,)), dma((2 * depth,)), dma((2 * depth,)),
         ],
         compiler_params=pltpu.CompilerParams(
             collective_id=0, has_side_effects=True, vmem_limit_bytes=48 * 2**20

time: 41.9 us -> 39.5 us (0.943)
  Pallas kernels: 36.7 us -> 34.2 us
    pallas_call x1, Pallas kernels: 36.7 us -> 34.2 us  [kernel_body(): pl.pallas_call(functools.partial(kernel, depth), out_shape=pltpu.VMEM((wi...]
where the time goes in v5:
time: 39.5 us; the launch traced here: 39.3 us
  Pallas kernels  34.2 us (87%)
  matrix products  4.79 us (12%)
    pallas_call x1, Pallas kernels, kernel_body(): pl.pallas_call(functools.partial(kernel, depth), out_shape=pltpu.VMEM((wi...  34.2 us
    dot_general x5, matrix products, newton_schulz(): jnp.einsum('hrv,hvw->hrw', ortho, poly, preferred_element_type=jnp.float32)  2.98 us
    dot_general x5, matrix products, newton_schulz(): jnp.einsum('hrv,hrw->hvw', ortho, ortho, preferred_element_type=jnp.float32)  1.81 us

profile of v5, /device:TPU:0, one launch (start us, length us, event | category | flops | bytes accessed | tf_op | source)
XLA Modules:
  0.0 39.3 jit_solution(8298163772444448112)
XLA Ops:
  0.0 34.2 %gradient_sums.1 = bf16[4,4,128,128]{3,2,1,0:T(8,128)(2,1)S(1)} custom-call(s32[8]{0:T(128)} %len_hbm.1, bf16[1536,128]{1,0:T(8,128)(2,1)} %lat_hbm.1, bf16[1536,512]{1,0:T(8,128)(2,1)} %vg_hbm.1), custom_call_target="tpu_custom_call" | custom-call | tf_op jit(solution)/shard_map/gradient_sums/pallas_call | solution.py:327
  34.2 0.2 multiply_reduce_fusion
  34.5 0.4 %fusion.20 = bf16[4,128,128]{2,1,0:T(8,128)(2,1)S(1)} fusion(bf16[4,512,128]{2,1,0:T(8,128)(2,1)S(1)} %bitcast.26, f32[4]{0:T(128)S(1)} %add_divide_fusion), kind=kOutput, calls=%fused_computation.35 | convolution fusion | flops 67305472 | bytes 655376 | tf_op jit(solution)/shard_map/hrv,hrw->hvw/dot_general | solution.py:67
  34.9 0.4 %fusion.1 = bf16[4,512,128]{2,1,0:T(8,128)(2,1)S(1)} fusion(bf16[4,512,128]{2,1,0:T(8,128)(2,1)S(1)} %bitcast.27, bf16[4,128,128]{2,1,0:T(8,128)(2,1)S(1)} %fusion.20, f32[4]{0:T(128)S(1)} %add_divide_fusion), kind=kOutput, calls=%fused_computation.6 | convolution fusion | flops 85524480 | bytes 1179664 | tf_op jit(solution)/shard_map/hrv,hvw->hrw/dot_general | solution.py:73
  35.3 0.3 convolution_convert_fusion.3
  35.7 0.4 %fusion.2 = bf16[4,512,128]{2,1,0:T(8,128)(2,1)S(1)} fusion(bf16[4,512,128]{2,1,0:T(8,128)(2,1)S(1)} %fusion.1, bf16[4,128,128]{2,1,0:T(8,128)(2,1)S(1)} %convolution_convert_fusion.3), kind=kOutput, calls=%fused_computation.7 | convolution fusion | flops 85262336 | bytes 1179648 | tf_op jit(solution)/shard_map/hrv,hvw->hrw/dot_general | solution.py:73
  36.1 0.3 convolution_convert_fusion.2
  36.5 0.4 %fusion.3 = bf16[4,512,128]{2,1,0:T(8,128)(2,1)S(1)} fusion(bf16[4,512,128]{2,1,0:T(8,128)(2,1)S(1)} %fusion.2, bf16[4,128,128]{2,1,0:T(8,128)(2,1)S(1)} %convolution_convert_fusion.2), kind=kOutput, calls=%fused_computation.8 | convolution fusion | flops 85262336 | bytes 1179648 | tf_op jit(solution)/shard_map/hrv,hvw->hrw/dot_general | solution.py:73
  36.9 0.3 convolution_convert_fusion.1
  37.3 0.4 %fusion.4 = bf16[4,512,128]{2,1,0:T(8,128)(2,1)S(1)} fusion(bf16[4,512,128]{2,1,0:T(8,128)(2,1)S(1)} %fusion.3, bf16[4,128,128]{2,1,0:T(8,128)(2,1)S(1)} %convolution_convert_fusion.1), kind=kOutput, calls=%fused_computation.9 | convolution fusion | flops 85262336 | bytes 1179648 | tf_op jit(solution)/shard_map/hrv,hvw->hrw/dot_general | solution.py:73
  37.7 0.3 convolution_convert_fusion
  38.1 1.2 %fusion.8 = bf16[4,512,128]{2,1,0:T(8,128)(2,1)} fusion(bf16[4,512,128]{2,1,0:T(8,128)(2,1)S(1)} %fusion.4, bf16[4,128,128]{2,1,0:T(8,128)(2,1)S(1)} %convolution_convert_fusion), kind=kOutput, calls=%fused_computation.13 | convolution fusion | flops 86048768 | bytes 1179648 | tf_op jit(solution)/shard_map/hrv,hvw->hrw/dot_general | solution.py:73
  (1 shorter events, 0.0 us)

commit v6 on v5

--- a/solution.py
+++ b/solution.py
@@ -271,28 +271,34 @@
         forward[i].start()
 
     last = len(units) - 1
+
+    def multiply_piece(i):
+        c, k = pieces[i]
+        forward[i].wait_recv()
+        multiply([2, 3], c * part_rows, part_rows, k)
+        if i == TOKEN_PARTS - 1:
+            swap(1).start()
+
     loads[2].wait()
-    multiply([0], 0, lat_cols)
     near.wait_recv()
-    multiply([1], 0, lat_cols)
+    for k in range(TOKEN_PARTS):
+        multiply([0, 1], 0, lat_cols, k)
+        if k == 0:
+            arrive(0)
     swap(0).start()
-    for c in range(ROW_PARTS):
-        for k in range(TOKEN_PARTS):
-            i = c * TOKEN_PARTS + k
-            arrive(i)
-            if k == 1:
-                stage_z(c)
-            if c == 1 and k == 2:
-                stage_gather(1)
-            forward[i].wait_recv()
-            multiply([2, 3], c * part_rows, part_rows, k)
-        if c == 0:
-            swap(1).start()
-            stage_gather(0)
+    for i in range(1, len(pieces)):
+        arrive(i)
+        multiply_piece(i - 1)
+        if i == len(pieces) - 2:
+            stage_z(0)
+    stage_z(1)
+    multiply_piece(len(pieces) - 1)
     for o in others:
         scatter_all(last, *o).start()
+    stage_gather(0)
+    stage_gather(1)
+    reduce_all(last)
     stage_share(0)
-    reduce_all(last)
     stage_share(1)
     for u in range(last):
         share(u).wait_recv()

time: 39.5 us -> 40.2 us (1.018)
  Pallas kernels: 34.2 us -> 35 us
    pallas_call x1, Pallas kernels: 34.2 us -> 35 us  [kernel_body(): pl.pallas_call(functools.partial(kernel, depth), out_shape=pltpu.VMEM((wi...]
where the time goes in v6:
time: 40.2 us; the launch traced here: 40.1 us
  Pallas kernels  35 us (87%)
  matrix products  4.79 us (12%)
    pallas_call x1, Pallas kernels, kernel_body(): pl.pallas_call(functools.partial(kernel, depth), out_shape=pltpu.VMEM((wi...  35 us
    dot_general x5, matrix products, newton_schulz(): jnp.einsum('hrv,hvw->hrw', ortho, poly, preferred_element_type=jnp.float32)  2.97 us
    dot_general x5, matrix products, newton_schulz(): jnp.einsum('hrv,hrw->hvw', ortho, ortho, preferred_element_type=jnp.float32)  1.82 us

profile of v6, /device:TPU:0, one launch (start us, length us, event | category | flops | bytes accessed | tf_op | source)
XLA Modules:
  0.0 40.1 jit_solution(4003799297506411815)
XLA Ops:
  0.0 35.0 %gradient_sums.1 = bf16[4,4,128,128]{3,2,1,0:T(8,128)(2,1)S(1)} custom-call(s32[8]{0:T(128)} %len_hbm.1, bf16[1536,128]{1,0:T(8,128)(2,1)} %lat_hbm.1, bf16[1536,512]{1,0:T(8,128)(2,1)} %vg_hbm.1), custom_call_target="tpu_custom_call" | custom-call | tf_op jit(solution)/shard_map/gradient_sums/pallas_call | solution.py:333
  35.0 0.2 multiply_reduce_fusion
  35.3 0.4 %fusion.20 = bf16[4,128,128]{2,1,0:T(8,128)(2,1)S(1)} fusion(bf16[4,512,128]{2,1,0:T(8,128)(2,1)S(1)} %bitcast.26, f32[4]{0:T(128)S(1)} %add_divide_fusion), kind=kOutput, calls=%fused_computation.35 | convolution fusion | flops 67305472 | bytes 655376 | tf_op jit(solution)/shard_map/hrv,hrw->hvw/dot_general | solution.py:67
  35.7 0.4 %fusion.1 = bf16[4,512,128]{2,1,0:T(8,128)(2,1)S(1)} fusion(bf16[4,512,128]{2,1,0:T(8,128)(2,1)S(1)} %bitcast.27, bf16[4,128,128]{2,1,0:T(8,128)(2,1)S(1)} %fusion.20, f32[4]{0:T(128)S(1)} %add_divide_fusion), kind=kOutput, calls=%fused_computation.6 | convolution fusion | flops 85524480 | bytes 1179664 | tf_op jit(solution)/shard_map/hrv,hvw->hrw/dot_general | solution.py:73
  36.1 0.4 convolution_convert_fusion.3
  36.5 0.4 %fusion.2 = bf16[4,512,128]{2,1,0:T(8,128)(2,1)S(1)} fusion(bf16[4,512,128]{2,1,0:T(8,128)(2,1)S(1)} %fusion.1, bf16[4,128,128]{2,1,0:T(8,128)(2,1)S(1)} %convolution_convert_fusion.3), kind=kOutput, calls=%fused_computation.7 | convolution fusion | flops 85262336 | bytes 1179648 | tf_op jit(solution)/shard_map/hrv,hvw->hrw/dot_general | solution.py:73
  36.9 0.4 convolution_convert_fusion.2
  37.3 0.4 %fusion.3 = bf16[4,512,128]{2,1,0:T(8,128)(2,1)S(1)} fusion(bf16[4,512,128]{2,1,0:T(8,128)(2,1)S(1)} %fusion.2, bf16[4,128,128]{2,1,0:T(8,128)(2,1)S(1)} %convolution_convert_fusion.2), kind=kOutput, calls=%fused_computation.8 | convolution fusion | flops 85262336 | bytes 1179648 | tf_op jit(solution)/shard_map/hrv,hvw->hrw/dot_general | solution.py:73
  37.7 0.4 convolution_convert_fusion.1
  38.1 0.4 %fusion.4 = bf16[4,512,128]{2,1,0:T(8,128)(2,1)S(1)} fusion(bf16[4,512,128]{2,1,0:T(8,128)(2,1)S(1)} %fusion.3, bf16[4,128,128]{2,1,0:T(8,128)(2,1)S(1)} %convolution_convert_fusion.1), kind=kOutput, calls=%fused_computation.9 | convolution fusion | flops 85262336 | bytes 1179648 | tf_op jit(solution)/shard_map/hrv,hvw->hrw/dot_general | solution.py:73
  38.5 0.4 convolution_convert_fusion
  38.9 1.2 %fusion.8 = bf16[4,512,128]{2,1,0:T(8,128)(2,1)} fusion(bf16[4,512,128]{2,1,0:T(8,128)(2,1)S(1)} %fusion.4, bf16[4,128,128]{2,1,0:T(8,128)(2,1)S(1)} %convolution_convert_fusion), kind=kOutput, calls=%fused_computation.13 | convolution fusion | flops 86048768 | bytes 1179648 | tf_op jit(solution)/shard_map/hrv,hvw->hrw/dot_general | solution.py:73
  (1 shorter events, 0.0 us)

commit v7 on v6

--- a/solution.py
+++ b/solution.py
@@ -213,7 +213,9 @@
     def gather_all(u, far_y, d):
         i = far_y * depth + d
         block = grad.at[(pl.ds(y * count, count),) + block_of(u, z)]
-        return remote(block, block, e_send.at[i], e_recv.at[i], (other_dp(far_y, d), head))
+        return remote(
+            block, block, e_send.at[u, i], e_recv.at[u, i], (other_dp(far_y, d), head)
+        )
 
     def multiply(s, row, rows, k=None):
         tokens = pl.ds(0, capacity) if k is None else pl.ds(k * span, span)
@@ -244,8 +246,12 @@
             scatter(u, d).wait_recv()
             total = total + zbuf[(d,) + buffer_of(u)].astype(jnp.float32)
         keep(u, total)
-        for d in range(1, depth):
-            gather(u, d).start()
+        if u == 0:
+            for d in range(1, depth):
+                gather(u, d).start()
+        else:
+            for o in others:
+                gather_all(u, *o).start()
 
     def keep(u, total):
         for h in range(count):
@@ -288,22 +294,22 @@
     swap(0).start()
     for i in range(1, len(pieces)):
         arrive(i)
+        if i == len(pieces) - 1:
+            stage_gather(0)
         multiply_piece(i - 1)
-        if i == len(pieces) - 2:
+        if i == len(pieces) // 2:
             stage_z(0)
     stage_z(1)
     multiply_piece(len(pieces) - 1)
     for o in others:
         scatter_all(last, *o).start()
-    stage_gather(0)
+    stage_share(0)
     stage_gather(1)
     reduce_all(last)
-    stage_share(0)
-    stage_share(1)
-    for u in range(last):
-        share(u).wait_recv()
-    for o in others:
-        gather_all(last, *o).wait_recv()
+    share(0).wait_recv()
+    for u in range(1, last + 1):
+        for o in others:
+            gather_all(u, *o).wait_recv()
 
     near.wait_send()
     for i in range(len(pieces)):
@@ -311,13 +317,15 @@
         forward[i].wait_send()
     for o in others:
         scatter_all(last, *o).wait_send()
-        gather_all(last, *o).wait_send()
+        for u in range(1, last + 1):
+            gather_all(u, *o).wait_send()
+    share(0).wait_send()
+    for d in range(1, depth):
+        gather(0, d).wait_send()
     for u in range(last):
         swap(u).wait_send()
-        share(u).wait_send()
         for d in range(1, depth):
             scatter(u, d).wait_send()
-            gather(u, d).wait_send()
 
 
 def kernel_body(depth, latent, value_grad, lengths):
@@ -353,7 +361,7 @@
             dma((units, depth)), dma((units, depth)),
             dma((units, depth)), dma((units, depth)),
             dma((units,)), dma((units,)),
-            dma((2 * depth,)), dma((2 * depth,)), dma((2 * depth,)), dma((2 * depth,)),
+            dma((2 * depth,)), dma((2 * depth,)), dma((1 + units, 2 * depth)), dma((1 + units, 2 * depth)),
         ],
         compiler_params=pltpu.CompilerParams(
             collective_id=0, has_side_effects=True, vmem_limit_bytes=48 * 2**20

time: 40.2 us -> 42.2 us (1.050)
  Pallas kernels: 35 us -> 37 us
    pallas_call x1, Pallas kernels: 35 us -> 37 us  [kernel_body(): pl.pallas_call(functools.partial(kernel, depth), out_shape=pltpu.VMEM((wi...]
where the time goes in v7:
time: 42.2 us; the launch traced here: 42 us
  Pallas kernels  37 us (88%)
  matrix products  4.79 us (11%)
    pallas_call x1, Pallas kernels, kernel_body(): pl.pallas_call(functools.partial(kernel, depth), out_shape=pltpu.VMEM((wi...  37 us
    dot_general x5, matrix products, newton_schulz(): jnp.einsum('hrv,hvw->hrw', ortho, poly, preferred_element_type=jnp.float32)  2.97 us
    dot_general x5, matrix products, newton_schulz(): jnp.einsum('hrv,hrw->hvw', ortho, ortho, preferred_element_type=jnp.float32)  1.82 us

profile of v7, /device:TPU:0, one launch (start us, length us, event | category | flops | bytes accessed | tf_op | source)
XLA Modules:
  0.0 42.0 jit_solution(4608201521557324703)
XLA Ops:
  0.0 37.0 %gradient_sums.1 = bf16[4,4,128,128]{3,2,1,0:T(8,128)(2,1)S(1)} custom-call(s32[8]{0:T(128)} %len_hbm.1, bf16[1536,128]{1,0:T(8,128)(2,1)} %lat_hbm.1, bf16[1536,512]{1,0:T(8,128)(2,1)} %vg_hbm.1), custom_call_target="tpu_custom_call" | custom-call | tf_op jit(solution)/shard_map/gradient_sums/pallas_call | solution.py:341
  37.0 0.2 multiply_reduce_fusion
  37.2 0.4 fusion.20
  37.6 0.4 %fusion.1 = bf16[4,512,128]{2,1,0:T(8,128)(2,1)S(1)} fusion(bf16[4,512,128]{2,1,0:T(8,128)(2,1)S(1)} %bitcast.27, bf16[4,128,128]{2,1,0:T(8,128)(2,1)S(1)} %fusion.20, f32[4]{0:T(128)S(1)} %add_divide_fusion), kind=kOutput, calls=%fused_computation.6 | convolution fusion | flops 85524480 | bytes 1179664 | tf_op jit(solution)/shard_map/hrv,hvw->hrw/dot_general | solution.py:73
  38.1 0.4 convolution_convert_fusion.3
  38.4 0.4 %fusion.2 = bf16[4,512,128]{2,1,0:T(8,128)(2,1)S(1)} fusion(bf16[4,512,128]{2,1,0:T(8,128)(2,1)S(1)} %fusion.1, bf16[4,128,128]{2,1,0:T(8,128)(2,1)S(1)} %convolution_convert_fusion.3), kind=kOutput, calls=%fused_computation.7 | convolution fusion | flops 85262336 | bytes 1179648 | tf_op jit(solution)/shard_map/hrv,hvw->hrw/dot_general | solution.py:73
  38.9 0.4 convolution_convert_fusion.2
  39.2 0.4 %fusion.3 = bf16[4,512,128]{2,1,0:T(8,128)(2,1)S(1)} fusion(bf16[4,512,128]{2,1,0:T(8,128)(2,1)S(1)} %fusion.2, bf16[4,128,128]{2,1,0:T(8,128)(2,1)S(1)} %convolution_convert_fusion.2), kind=kOutput, calls=%fused_computation.8 | convolution fusion | flops 85262336 | bytes 1179648 | tf_op jit(solution)/shard_map/hrv,hvw->hrw/dot_general | solution.py:73
  39.6 0.4 convolution_convert_fusion.1
  40.0 0.4 %fusion.4 = bf16[4,512,128]{2,1,0:T(8,128)(2,1)S(1)} fusion(bf16[4,512,128]{2,1,0:T(8,128)(2,1)S(1)} %fusion.3, bf16[4,128,128]{2,1,0:T(8,128)(2,1)S(1)} %convolution_convert_fusion.1), kind=kOutput, calls=%fused_computation.9 | convolution fusion | flops 85262336 | bytes 1179648 | tf_op jit(solution)/shard_map/hrv,hvw->hrw/dot_general | solution.py:73
  40.4 0.4 convolution_convert_fusion
  40.8 1.2 %fusion.8 = bf16[4,512,128]{2,1,0:T(8,128)(2,1)} fusion(bf16[4,512,128]{2,1,0:T(8,128)(2,1)S(1)} %fusion.4, bf16[4,128,128]{2,1,0:T(8,128)(2,1)S(1)} %convolution_convert_fusion), kind=kOutput, calls=%fused_computation.13 | convolution fusion | flops 86048768 | bytes 1179648 | tf_op jit(solution)/shard_map/hrv,hvw->hrw/dot_general | solution.py:73
  (1 shorter events, 0.0 us)

commit v8 on v6

--- a/solution.py
+++ b/solution.py
@@ -162,8 +162,7 @@
     for k in range(1, TOKEN_PARTS):
         turn(k)
     near.start()
-    for c in over[1:]:
-        c.start()
+    over[1].start()
 
     own, other = head - core, partner - core
     units = [(own, 0, lat_cols)]
@@ -269,6 +268,8 @@
     def arrive(i):
         over[i].wait_recv()
         forward[i].start()
+        if i + 2 < len(pieces):
+            over[i + 2].start()
 
     last = len(units) - 1
 

time: 40.2 us -> 39.8 us (0.990)
  Pallas kernels: 35 us -> 34.5 us
    pallas_call x1, Pallas kernels: 35 us -> 34.5 us  [kernel_body(): pl.pallas_call(functools.partial(kernel, depth), out_shape=pltpu.VMEM((wi...]
where the time goes in v8:
time: 39.8 us; the launch traced here: 39.6 us
  Pallas kernels  34.5 us (87%)
  matrix products  4.8 us (12%)
    pallas_call x1, Pallas kernels, kernel_body(): pl.pallas_call(functools.partial(kernel, depth), out_shape=pltpu.VMEM((wi...  34.5 us
    dot_general x5, matrix products, newton_schulz(): jnp.einsum('hrv,hvw->hrw', ortho, poly, preferred_element_type=jnp.float32)  2.98 us
    dot_general x5, matrix products, newton_schulz(): jnp.einsum('hrv,hrw->hvw', ortho, ortho, preferred_element_type=jnp.float32)  1.82 us

profile of v8, /device:TPU:0, one launch (start us, length us, event | category | flops | bytes accessed | tf_op | source)
XLA Modules:
  0.0 39.6 jit_solution(1286981938507071611)
XLA Ops:
  0.0 34.5 %gradient_sums.1 = bf16[4,4,128,128]{3,2,1,0:T(8,128)(2,1)S(1)} custom-call(s32[8]{0:T(128)} %len_hbm.1, bf16[1536,128]{1,0:T(8,128)(2,1)} %lat_hbm.1, bf16[1536,512]{1,0:T(8,128)(2,1)} %vg_hbm.1), custom_call_target="tpu_custom_call" | custom-call | tf_op jit(solution)/shard_map/gradient_sums/pallas_call | solution.py:334
  34.5 0.2 multiply_reduce_fusion
  34.8 0.4 %fusion.20 = bf16[4,128,128]{2,1,0:T(8,128)(2,1)S(1)} fusion(bf16[4,512,128]{2,1,0:T(8,128)(2,1)S(1)} %bitcast.26, f32[4]{0:T(128)S(1)} %add_divide_fusion), kind=kOutput, calls=%fused_computation.35 | convolution fusion | flops 67305472 | bytes 655376 | tf_op jit(solution)/shard_map/hrv,hrw->hvw/dot_general | solution.py:67
  35.2 0.4 %fusion.1 = bf16[4,512,128]{2,1,0:T(8,128)(2,1)S(1)} fusion(bf16[4,512,128]{2,1,0:T(8,128)(2,1)S(1)} %bitcast.27, bf16[4,128,128]{2,1,0:T(8,128)(2,1)S(1)} %fusion.20, f32[4]{0:T(128)S(1)} %add_divide_fusion), kind=kOutput, calls=%fused_computation.6 | convolution fusion | flops 85524480 | bytes 1179664 | tf_op jit(solution)/shard_map/hrv,hvw->hrw/dot_general | solution.py:73
  35.6 0.4 convolution_convert_fusion.3
  36.0 0.4 %fusion.2 = bf16[4,512,128]{2,1,0:T(8,128)(2,1)S(1)} fusion(bf16[4,512,128]{2,1,0:T(8,128)(2,1)S(1)} %fusion.1, bf16[4,128,128]{2,1,0:T(8,128)(2,1)S(1)} %convolution_convert_fusion.3), kind=kOutput, calls=%fused_computation.7 | convolution fusion | flops 85262336 | bytes 1179648 | tf_op jit(solution)/shard_map/hrv,hvw->hrw/dot_general | solution.py:73
  36.4 0.3 convolution_convert_fusion.2
  36.8 0.4 %fusion.3 = bf16[4,512,128]{2,1,0:T(8,128)(2,1)S(1)} fusion(bf16[4,512,128]{2,1,0:T(8,128)(2,1)S(1)} %fusion.2, bf16[4,128,128]{2,1,0:T(8,128)(2,1)S(1)} %convolution_convert_fusion.2), kind=kOutput, calls=%fused_computation.8 | convolution fusion | flops 85262336 | bytes 1179648 | tf_op jit(solution)/shard_map/hrv,hvw->hrw/dot_general | solution.py:73
  37.2 0.3 convolution_convert_fusion.1
  37.6 0.4 %fusion.4 = bf16[4,512,128]{2,1,0:T(8,128)(2,1)S(1)} fusion(bf16[4,512,128]{2,1,0:T(8,128)(2,1)S(1)} %fusion.3, bf16[4,128,128]{2,1,0:T(8,128)(2,1)S(1)} %convolution_convert_fusion.1), kind=kOutput, calls=%fused_computation.9 | convolution fusion | flops 85262336 | bytes 1179648 | tf_op jit(solution)/shard_map/hrv,hvw->hrw/dot_general | solution.py:73
  38.0 0.3 convolution_convert_fusion
  38.4 1.2 %fusion.8 = bf16[4,512,128]{2,1,0:T(8,128)(2,1)} fusion(bf16[4,512,128]{2,1,0:T(8,128)(2,1)S(1)} %fusion.4, bf16[4,128,128]{2,1,0:T(8,128)(2,1)S(1)} %convolution_convert_fusion), kind=kOutput, calls=%fused_computation.13 | convolution fusion | flops 86048768 | bytes 1179648 | tf_op jit(solution)/shard_map/hrv,hvw->hrw/dot_general | solution.py:73
  (1 shorter events, 0.0 us)

commit v9 on v8

--- a/solution.py
+++ b/solution.py
@@ -82,9 +82,8 @@
 def kernel(
     depth,
     len_hbm, lat_hbm, vg_hbm, grad,
-    len_s, lat_v, vg_v, lat_t, acc, part, ybuf, zacc, zpart, zbuf, dbuf,
+    len_s, lat_v, vg_v, lat_t, acc, part, dbuf,
     load_sem, sib_sem, x_send, x_recv, f_send, f_recv,
-    y_send, y_recv, z_send, z_recv, a_send, a_recv, b_send, b_recv,
     d_send, d_recv, e_send, e_recv,
 ):
     dp = lax.axis_index("dp")
@@ -95,15 +94,11 @@
     partner = lax.rem(head + 2, 4)
     far = lax.rem(sibling + 2, 4)
     source = (head, sibling, partner, far)
-    across = dp + 1 - 2 * y
     lat_cols, capacity = lat_t.shape[1], lat_t.shape[2]
     half = acc.shape[3]
     count = half // V_DIM
     part_rows = lat_cols // ROW_PARTS
     span = capacity // TOKEN_PARTS
-
-    def along(d):
-        return lax.rem(z + d, depth) * 2 + y
 
     def side(far_y):
         return 1 - y if far_y else y
@@ -168,10 +163,6 @@
     units = [(own, 0, lat_cols)]
     units += [(other, c * part_rows, part_rows) for c in range(ROW_PARTS)]
 
-    def rows_of(u):
-        s, row, rows = units[u]
-        return pl.ds(s, 2), pl.ds(row, rows)
-
     def block_of(u, zz):
         s, row, rows = units[u]
         block = rows // depth
@@ -181,38 +172,17 @@
         s, row, rows = units[u]
         return pl.ds(s, 2), pl.ds(row // depth, rows // depth)
 
-    def swap(u):
-        slots, here = rows_of(u)
-        return remote(
-            part.at[1 - y, slots, here], ybuf.at[slots, here],
-            y_send.at[u], y_recv.at[u], (across, head),
-        )
-
-    def scatter(u, d):
-        return remote(
-            zpart.at[block_of(u, lax.rem(z + d, depth))], zbuf.at[(d,) + buffer_of(u)],
-            z_send.at[u, d], z_recv.at[u, d], (along(d), head),
-        )
-
-    def gather(u, d):
-        block = grad.at[(pl.ds(y * count, count),) + block_of(u, z)]
-        return remote(block, block, a_send.at[u, d], a_recv.at[u, d], (along(d), head))
-
-    def share(u):
-        block = grad.at[(pl.ds(y * count, count),) + rows_of(u)]
-        return remote(block, block, b_send.at[u], b_recv.at[u], (across, head))
-
     def scatter_all(u, far_y, d):
         i = far_y * depth + d
         return remote(
-            part.at[(side(far_y),) + block_of(u, lax.rem(z + d, depth))], dbuf.at[i],
-            d_send.at[i], d_recv.at[i], (other_dp(far_y, d), head),
+            part.at[(side(far_y),) + block_of(u, lax.rem(z + d, depth))], dbuf.at[(i,) + buffer_of(u)],
+            d_send.at[u, i], d_recv.at[u, i], (other_dp(far_y, d), head),
         )
 
     def gather_all(u, far_y, d):
         i = far_y * depth + d
         block = grad.at[(pl.ds(y * count, count),) + block_of(u, z)]
-        return remote(block, block, e_send.at[i], e_recv.at[i], (other_dp(far_y, d), head))
+        return remote(block, block, e_send.at[u, i], e_recv.at[u, i], (other_dp(far_y, d), head))
 
     def multiply(s, row, rows, k=None):
         tokens = pl.ds(0, capacity) if k is None else pl.ds(k * span, span)
@@ -228,24 +198,6 @@
                 if k is None or k == TOKEN_PARTS - 1:
                     part[j, source[i], here, :] = mine.astype(jnp.bfloat16)
 
-    def stage_z(u):
-        here = rows_of(u)
-        swap(u).wait_recv()
-        total = acc[(y,) + here] + ybuf[here].astype(jnp.float32)
-        zacc[here] = total
-        zpart[here] = total.astype(jnp.bfloat16)
-        for d in range(1, depth):
-            scatter(u, d).start()
-
-    def stage_gather(u):
-        total = zacc[block_of(u, z)]
-        for d in range(1, depth):
-            scatter(u, d).wait_recv()
-            total = total + zbuf[(d,) + buffer_of(u)].astype(jnp.float32)
-        keep(u, total)
-        for d in range(1, depth):
-            gather(u, d).start()
-
     def keep(u, total):
         for h in range(count):
             columns = total[..., h * V_DIM : (h + 1) * V_DIM]
@@ -255,15 +207,10 @@
         total = acc[(y,) + block_of(u, z)]
         for o in others:
             scatter_all(u, *o).wait_recv()
-            total = total + dbuf[o[0] * depth + o[1]].astype(jnp.float32)
+            total = total + dbuf[(o[0] * depth + o[1],) + buffer_of(u)].astype(jnp.float32)
         keep(u, total)
         for o in others:
             gather_all(u, *o).start()
-
-    def stage_share(u):
-        for d in range(1, depth):
-            gather(u, d).wait_recv()
-        share(u).start()
 
     def arrive(i):
         over[i].wait_recv()
@@ -271,14 +218,16 @@
         if i + 2 < len(pieces):
             over[i + 2].start()
 
-    last = len(units) - 1
+    def scatter_unit(u):
+        for o in others:
+            scatter_all(u, *o).start()
 
     def multiply_piece(i):
         c, k = pieces[i]
         forward[i].wait_recv()
         multiply([2, 3], c * part_rows, part_rows, k)
         if i == TOKEN_PARTS - 1:
-            swap(1).start()
+            scatter_unit(1)
 
     loads[2].wait()
     near.wait_recv()
@@ -286,46 +235,35 @@
         multiply([0, 1], 0, lat_cols, k)
         if k == 0:
             arrive(0)
-    swap(0).start()
+    scatter_unit(0)
     for i in range(1, len(pieces)):
         arrive(i)
         multiply_piece(i - 1)
         if i == len(pieces) - 2:
-            stage_z(0)
-    stage_z(1)
+            reduce_all(0)
     multiply_piece(len(pieces) - 1)
-    for o in others:
-        scatter_all(last, *o).start()
-    stage_gather(0)
-    stage_gather(1)
-    reduce_all(last)
-    stage_share(0)
-    stage_share(1)
-    for u in range(last):
-        share(u).wait_recv()
-    for o in others:
-        gather_all(last, *o).wait_recv()
+    scatter_unit(2)
+    reduce_all(1)
+    reduce_all(2)
+    for u in range(len(units)):
+        for o in others:
+            gather_all(u, *o).wait_recv()
 
     near.wait_send()
     for i in range(len(pieces)):
         over[i].wait_send()
         forward[i].wait_send()
-    for o in others:
-        scatter_all(last, *o).wait_send()
-        gather_all(last, *o).wait_send()
-    for u in range(last):
-        swap(u).wait_send()
-        share(u).wait_send()
-        for d in range(1, depth):
-            scatter(u, d).wait_send()
-            gather(u, d).wait_send()
+    for u in range(len(units)):
+        for o in others:
+            scatter_all(u, *o).wait_send()
+            gather_all(u, *o).wait_send()
 
 
 def kernel_body(depth, latent, value_grad, lengths):
     capacity, lat_cols = latent.shape
     width = value_grad.shape[1]
     half = width // 2
-    units, pieces = ROW_PARTS, ROW_PARTS * TOKEN_PARTS
+    units, pieces = 1 + ROW_PARTS, ROW_PARTS * TOKEN_PARTS
     dma = pltpu.SemaphoreType.DMA
     low, full = jnp.bfloat16, jnp.float32
     latent, value_grad, lengths = (
@@ -343,18 +281,10 @@
             pltpu.VMEM((4, lat_cols, capacity), low),
             pltpu.VMEM((2, 4, lat_cols, half), full),
             pltpu.VMEM((2, 4, lat_cols, half), low),
-            pltpu.VMEM((4, lat_cols, half), low),
-            pltpu.VMEM((4, lat_cols, half), full),
-            pltpu.VMEM((4, lat_cols, half), low),
-            pltpu.VMEM((depth, 4, lat_cols // depth, half), low),
-            pltpu.VMEM((2 * depth, 2, lat_cols // ROW_PARTS // depth, half), low),
+            pltpu.VMEM((2 * depth, 4, lat_cols // depth, half), low),
             dma((3,)), dma((2,)),
             dma((pieces,)), dma((pieces,)), dma((pieces,)), dma((pieces,)),
-            dma((units,)), dma((units,)),
-            dma((units, depth)), dma((units, depth)),
-            dma((units, depth)), dma((units, depth)),
-            dma((units,)), dma((units,)),
-            dma((2 * depth,)), dma((2 * depth,)), dma((2 * depth,)), dma((2 * depth,)),
+            dma((units, 2 * depth)), dma((units, 2 * depth)), dma((units, 2 * depth)), dma((units, 2 * depth)),
         ],
         compiler_params=pltpu.CompilerParams(
             collective_id=0, has_side_effects=True, vmem_limit_bytes=48 * 2**20

time: 39.8 us -> 41.1 us (1.033)
  Pallas kernels: 34.5 us -> 35.9 us
    pallas_call x1, Pallas kernels: 34.5 us -> 35.9 us  [kernel_body(): pl.pallas_call(functools.partial(kernel, depth), out_shape=pltpu.VMEM((wi...]
where the time goes in v9:
time: 41.1 us; the launch traced here: 41 us
  Pallas kernels  35.9 us (87%)
  matrix products  4.79 us (12%)
    pallas_call x1, Pallas kernels, kernel_body(): pl.pallas_call(functools.partial(kernel, depth), out_shape=pltpu.VMEM((wi...  35.9 us
    dot_general x5, matrix products, newton_schulz(): jnp.einsum('hrv,hvw->hrw', ortho, poly, preferred_element_type=jnp.float32)  2.97 us
    dot_general x5, matrix products, newton_schulz(): jnp.einsum('hrv,hrw->hvw', ortho, ortho, preferred_element_type=jnp.float32)  1.82 us

profile of v9, /device:TPU:0, one launch (start us, length us, event | category | flops | bytes accessed | tf_op | source)
XLA Modules:
  0.0 41.0 jit_solution(4643850844645280498)
XLA Ops:
  0.0 35.9 %gradient_sums.1 = bf16[4,4,128,128]{3,2,1,0:T(8,128)(2,1)S(1)} custom-call(s32[8]{0:T(128)} %len_hbm.1, bf16[1536,128]{1,0:T(8,128)(2,1)} %lat_hbm.1, bf16[1536,512]{1,0:T(8,128)(2,1)} %vg_hbm.1), custom_call_target="tpu_custom_call" | custom-call | tf_op jit(solution)/shard_map/gradient_sums/pallas_call | solution.py:272
  35.9 0.2 multiply_reduce_fusion
  36.1 0.4 %fusion.20 = bf16[4,128,128]{2,1,0:T(8,128)(2,1)S(1)} fusion(bf16[4,512,128]{2,1,0:T(8,128)(2,1)S(1)} %bitcast.26, f32[4]{0:T(128)S(1)} %add_divide_fusion), kind=kOutput, calls=%fused_computation.35 | convolution fusion | flops 67305472 | bytes 655376 | tf_op jit(solution)/shard_map/hrv,hrw->hvw/dot_general | solution.py:67
  36.5 0.4 %fusion.1 = bf16[4,512,128]{2,1,0:T(8,128)(2,1)S(1)} fusion(bf16[4,512,128]{2,1,0:T(8,128)(2,1)S(1)} %bitcast.27, bf16[4,128,128]{2,1,0:T(8,128)(2,1)S(1)} %fusion.20, f32[4]{0:T(128)S(1)} %add_divide_fusion), kind=kOutput, calls=%fused_computation.6 | convolution fusion | flops 85524480 | bytes 1179664 | tf_op jit(solution)/shard_map/hrv,hvw->hrw/dot_general | solution.py:73
  37.0 0.4 convolution_convert_fusion.3
  37.3 0.4 %fusion.2 = bf16[4,512,128]{2,1,0:T(8,128)(2,1)S(1)} fusion(bf16[4,512,128]{2,1,0:T(8,128)(2,1)S(1)} %fusion.1, bf16[4,128,128]{2,1,0:T(8,128)(2,1)S(1)} %convolution_convert_fusion.3), kind=kOutput, calls=%fused_computation.7 | convolution fusion | flops 85262336 | bytes 1179648 | tf_op jit(solution)/shard_map/hrv,hvw->hrw/dot_general | solution.py:73
  37.8 0.4 convolution_convert_fusion.2
  38.1 0.4 %fusion.3 = bf16[4,512,128]{2,1,0:T(8,128)(2,1)S(1)} fusion(bf16[4,512,128]{2,1,0:T(8,128)(2,1)S(1)} %fusion.2, bf16[4,128,128]{2,1,0:T(8,128)(2,1)S(1)} %convolution_convert_fusion.2), kind=kOutput, calls=%fused_computation.8 | convolution fusion | flops 85262336 | bytes 1179648 | tf_op jit(solution)/shard_map/hrv,hvw->hrw/dot_general | solution.py:73
  38.6 0.4 convolution_convert_fusion.1
  38.9 0.4 %fusion.4 = bf16[4,512,128]{2,1,0:T(8,128)(2,1)S(1)} fusion(bf16[4,512,128]{2,1,0:T(8,128)(2,1)S(1)} %fusion.3, bf16[4,128,128]{2,1,0:T(8,128)(2,1)S(1)} %convolution_convert_fusion.1), kind=kOutput, calls=%fused_computation.9 | convolution fusion | flops 85262336 | bytes 1179648 | tf_op jit(solution)/shard_map/hrv,hvw->hrw/dot_general | solution.py:73
  39.4 0.4 convolution_convert_fusion
  39.7 1.2 %fusion.8 = bf16[4,512,128]{2,1,0:T(8,128)(2,1)} fusion(bf16[4,512,128]{2,1,0:T(8,128)(2,1)S(1)} %fusion.4, bf16[4,128,128]{2,1,0:T(8,128)(2,1)S(1)} %convolution_convert_fusion), kind=kOutput, calls=%fused_computation.13 | convolution fusion | flops 86048768 | bytes 1179648 | tf_op jit(solution)/shard_map/hrv,hvw->hrw/dot_general | solution.py:73
  (1 shorter events, 0.0 us)

commit v10 on v5

--- a/solution.py
+++ b/solution.py
@@ -81,8 +81,8 @@
 
 def kernel(
     depth,
-    len_hbm, lat_hbm, vg_hbm, grad,
-    len_s, lat_v, vg_v, lat_t, acc, part, ybuf, zacc, zpart, zbuf, dbuf,
+    len_hbm, lat_hbm, vg_hbm, out_ref,
+    len_s, lat_v, vg_v, lat_t, acc, part, ybuf, zacc, zpart, zbuf, dbuf, grad,
     load_sem, sib_sem, x_send, x_recv, f_send, f_recv,
     y_send, y_recv, z_send, z_recv, a_send, a_recv, b_send, b_recv,
     d_send, d_recv, e_send, e_recv,
@@ -196,11 +196,11 @@
         )
 
     def gather(u, d):
-        block = grad.at[(pl.ds(y * count, count),) + block_of(u, z)]
+        block = grad.at[(y,) + block_of(u, z)]
         return remote(block, block, a_send.at[u, d], a_recv.at[u, d], (along(d), head))
 
     def share(u):
-        block = grad.at[(pl.ds(y * count, count),) + rows_of(u)]
+        block = grad.at[(y,) + rows_of(u)]
         return remote(block, block, b_send.at[u], b_recv.at[u], (across, head))
 
     def scatter_all(u, far_y, d):
@@ -212,7 +212,7 @@
 
     def gather_all(u, far_y, d):
         i = far_y * depth + d
-        block = grad.at[(pl.ds(y * count, count),) + block_of(u, z)]
+        block = grad.at[(y,) + block_of(u, z)]
         return remote(block, block, e_send.at[i], e_recv.at[i], (other_dp(far_y, d), head))
 
     def multiply(s, row, rows, k=None):
@@ -248,9 +248,7 @@
             gather(u, d).start()
 
     def keep(u, total):
-        for h in range(count):
-            columns = total[..., h * V_DIM : (h + 1) * V_DIM]
-            grad[(y * count + h,) + block_of(u, z)] = columns.astype(jnp.bfloat16)
+        grad[(y,) + block_of(u, z)] = total.astype(jnp.bfloat16)
 
     def reduce_all(u):
         total = acc[(y,) + block_of(u, z)]
@@ -298,6 +296,9 @@
         share(u).wait_recv()
     for o in others:
         gather_all(last, *o).wait_recv()
+    for j in range(2):
+        for h in range(count):
+            out_ref[j * count + h] = grad[j, :, :, pl.ds(h * V_DIM, V_DIM)]
 
     near.wait_send()
     for i in range(len(pieces)):
@@ -341,6 +342,7 @@
             pltpu.VMEM((4, lat_cols, half), low),
             pltpu.VMEM((depth, 4, lat_cols // depth, half), low),
             pltpu.VMEM((2 * depth, 2, lat_cols // ROW_PARTS // depth, half), low),
+            pltpu.VMEM((2, 4, lat_cols, half), low),
             dma((3,)), dma((2,)),
             dma((pieces,)), dma((pieces,)), dma((pieces,)), dma((pieces,)),
             dma((units,)), dma((units,)),

time: 39.5 us -> 39.5 us (level)
  no operation moved by 1% of the time
where the time goes in v10:
time: 39.5 us; the launch traced here: 39.4 us
  Pallas kernels  34.3 us (87%)
  matrix products  4.79 us (12%)
    pallas_call x1, Pallas kernels, kernel_body(): pl.pallas_call(functools.partial(kernel, depth), out_shape=pltpu.VMEM((wi...  34.3 us
    dot_general x5, matrix products, newton_schulz(): jnp.einsum('hrv,hvw->hrw', ortho, poly, preferred_element_type=jnp.float32)  2.98 us
    dot_general x5, matrix products, newton_schulz(): jnp.einsum('hrv,hrw->hvw', ortho, ortho, preferred_element_type=jnp.float32)  1.81 us

profile of v10, /device:TPU:0, one launch (start us, length us, event | category | flops | bytes accessed | tf_op | source)
XLA Modules:
  0.0 39.4 jit_solution(10192150071230240838)
XLA Ops:
  0.0 34.3 %gradient_sums.1 = bf16[4,4,128,128]{3,2,1,0:T(8,128)(2,1)S(1)} custom-call(s32[8]{0:T(128)} %len_hbm.1, bf16[1536,128]{1,0:T(8,128)(2,1)} %lat_hbm.1, bf16[1536,512]{1,0:T(8,128)(2,1)} %vg_hbm.1), custom_call_target="tpu_custom_call" | custom-call | tf_op jit(solution)/shard_map/gradient_sums/pallas_call | solution.py:328
  34.3 0.2 multiply_reduce_fusion
  34.6 0.4 %fusion.20 = bf16[4,128,128]{2,1,0:T(8,128)(2,1)S(1)} fusion(bf16[4,512,128]{2,1,0:T(8,128)(2,1)S(1)} %bitcast.26, f32[4]{0:T(128)S(1)} %add_divide_fusion), kind=kOutput, calls=%fused_computation.35 | convolution fusion | flops 67305472 | bytes 655376 | tf_op jit(solution)/shard_map/hrv,hrw->hvw/dot_general | solution.py:67
  35.0 0.4 %fusion.1 = bf16[4,512,128]{2,1,0:T(8,128)(2,1)S(1)} fusion(bf16[4,512,128]{2,1,0:T(8,128)(2,1)S(1)} %bitcast.27, bf16[4,128,128]{2,1,0:T(8,128)(2,1)S(1)} %fusion.20, f32[4]{0:T(128)S(1)} %add_divide_fusion), kind=kOutput, calls=%fused_computation.6 | convolution fusion | flops 85524480 | bytes 1179664 | tf_op jit(solution)/shard_map/hrv,hvw->hrw/dot_general | solution.py:73
  35.4 0.3 convolution_convert_fusion.3
  35.8 0.4 %fusion.2 = bf16[4,512,128]{2,1,0:T(8,128)(2,1)S(1)} fusion(bf16[4,512,128]{2,1,0:T(8,128)(2,1)S(1)} %fusion.1, bf16[4,128,128]{2,1,0:T(8,128)(2,1)S(1)} %convolution_convert_fusion.3), kind=kOutput, calls=%fused_computation.7 | convolution fusion | flops 85262336 | bytes 1179648 | tf_op jit(solution)/shard_map/hrv,hvw->hrw/dot_general | solution.py:73
  36.2 0.3 convolution_convert_fusion.2
  36.6 0.4 %fusion.3 = bf16[4,512,128]{2,1,0:T(8,128)(2,1)S(1)} fusion(bf16[4,512,128]{2,1,0:T(8,128)(2,1)S(1)} %fusion.2, bf16[4,128,128]{2,1,0:T(8,128)(2,1)S(1)} %convolution_convert_fusion.2), kind=kOutput, calls=%fused_computation.8 | convolution fusion | flops 85262336 | bytes 1179648 | tf_op jit(solution)/shard_map/hrv,hvw->hrw/dot_general | solution.py:73
  37.0 0.3 convolution_convert_fusion.1
  37.4 0.4 %fusion.4 = bf16[4,512,128]{2,1,0:T(8,128)(2,1)S(1)} fusion(bf16[4,512,128]{2,1,0:T(8,128)(2,1)S(1)} %fusion.3, bf16[4,128,128]{2,1,0:T(8,128)(2,1)S(1)} %convolution_convert_fusion.1), kind=kOutput, calls=%fused_computation.9 | convolution fusion | flops 85262336 | bytes 1179648 | tf_op jit(solution)/shard_map/hrv,hvw->hrw/dot_general | solution.py:73
  37.8 0.3 convolution_convert_fusion
  38.2 1.2 %fusion.8 = bf16[4,512,128]{2,1,0:T(8,128)(2,1)} fusion(bf16[4,512,128]{2,1,0:T(8,128)(2,1)S(1)} %fusion.4, bf16[4,128,128]{2,1,0:T(8,128)(2,1)S(1)} %convolution_convert_fusion), kind=kOutput, calls=%fused_computation.13 | convolution fusion | flops 86048768 | bytes 1179648 | tf_op jit(solution)/shard_map/hrv,hvw->hrw/dot_general | solution.py:73
  (1 shorter events, 0.0 us)

commit v11 on v10

--- a/solution.py
+++ b/solution.py
@@ -100,10 +100,14 @@
     half = acc.shape[3]
     count = half // V_DIM
     part_rows = lat_cols // ROW_PARTS
-    span = capacity // TOKEN_PARTS
+    tail = capacity // 6
+    span = (capacity - tail) // (TOKEN_PARTS - 1)
 
     def along(d):
         return lax.rem(z + d, depth) * 2 + y
+
+    def cut(k):
+        return pl.ds(k * span, span if k < TOKEN_PARTS - 1 else tail)
 
     def side(far_y):
         return 1 - y if far_y else y
@@ -129,7 +133,7 @@
     loads[1].wait()
 
     def turn(k):
-        tokens = pl.ds(k * span, span)
+        tokens = cut(k)
         turned = lat_v[tokens, :].T
         live = lax.broadcasted_iota(jnp.int32, turned.shape, 1) + k * span < len_s[dp]
         lat_t[0, :, tokens] = jnp.where(live, turned, jnp.zeros_like(turned))
@@ -147,7 +151,7 @@
 
     def piece(slot, i):
         c, k = pieces[i]
-        return lat_t.at[slot, pl.ds(c * part_rows, part_rows), pl.ds(k * span, span)]
+        return lat_t.at[slot, pl.ds(c * part_rows, part_rows), cut(k)]
 
     over = [
         remote(piece(0, i), piece(2, i), x_send.at[i], x_recv.at[i], (dp, partner))
@@ -216,7 +220,7 @@
         return remote(block, block, e_send.at[i], e_recv.at[i], (other_dp(far_y, d), head))
 
     def multiply(s, row, rows, k=None):
-        tokens = pl.ds(0, capacity) if k is None else pl.ds(k * span, span)
+        tokens = pl.ds(0, capacity) if k is None else cut(k)
         here = pl.ds(row, rows)
         lhs = jnp.concatenate([lat_t[i, here, tokens] for i in s], axis=0)
         for j in range(2):
@@ -274,22 +278,29 @@
     near.wait_recv()
     multiply([1], 0, lat_cols)
     swap(0).start()
-    for c in range(ROW_PARTS):
-        for k in range(TOKEN_PARTS):
-            i = c * TOKEN_PARTS + k
-            arrive(i)
-            if k == 1:
-                stage_z(c)
-            if c == 1 and k == 2:
-                stage_gather(1)
-            forward[i].wait_recv()
-            multiply([2, 3], c * part_rows, part_rows, k)
-        if c == 0:
+
+    def multiply_piece(i):
+        c, k = pieces[i]
+        forward[i].wait_recv()
+        multiply([2, 3], c * part_rows, part_rows, k)
+        if i == TOKEN_PARTS - 1:
             swap(1).start()
+
+    arrive(0)
+    for i in range(1, len(pieces)):
+        arrive(i)
+        if i == 1:
+            stage_z(0)
+        if i == len(pieces) - 1:
+            stage_z(1)
+        multiply_piece(i - 1)
+        if i == TOKEN_PARTS:
             stage_gather(0)
+    multiply_piece(len(pieces) - 1)
     for o in others:
         scatter_all(last, *o).start()
     stage_share(0)
+    stage_gather(1)
     reduce_all(last)
     stage_share(1)
     for u in range(last):

time: 39.5 us -> 38.7 us (0.980)
  Pallas kernels: 34.3 us -> 33.5 us
    pallas_call x1, Pallas kernels: 34.3 us -> 33.5 us  [kernel_body(): pl.pallas_call(functools.partial(kernel, depth), out_shape=pltpu.VMEM((wi...]
where the time goes in v11:
time: 38.7 us; the launch traced here: 38.6 us
  Pallas kernels  33.5 us (87%)
  matrix products  4.8 us (12%)
    pallas_call x1, Pallas kernels, kernel_body(): pl.pallas_call(functools.partial(kernel, depth), out_shape=pltpu.VMEM((wi...  33.5 us
    dot_general x5, matrix products, newton_schulz(): jnp.einsum('hrv,hvw->hrw', ortho, poly, preferred_element_type=jnp.float32)  2.98 us
    dot_general x5, matrix products, newton_schulz(): jnp.einsum('hrv,hrw->hvw', ortho, ortho, preferred_element_type=jnp.float32)  1.82 us

profile of v11, /device:TPU:0, one launch (start us, length us, event | category | flops | bytes accessed | tf_op | source)
XLA Modules:
  0.0 38.6 jit_solution(2384745121798742533)
XLA Ops:
  0.0 33.5 %gradient_sums.1 = bf16[4,4,128,128]{3,2,1,0:T(8,128)(2,1)S(1)} custom-call(s32[8]{0:T(128)} %len_hbm.1, bf16[1536,128]{1,0:T(8,128)(2,1)} %lat_hbm.1, bf16[1536,512]{1,0:T(8,128)(2,1)} %vg_hbm.1), custom_call_target="tpu_custom_call" | custom-call | tf_op jit(solution)/shard_map/gradient_sums/pallas_call | solution.py:339
  33.5 0.2 multiply_reduce_fusion
  33.8 0.4 %fusion.20 = bf16[4,128,128]{2,1,0:T(8,128)(2,1)S(1)} fusion(bf16[4,512,128]{2,1,0:T(8,128)(2,1)S(1)} %bitcast.26, f32[4]{0:T(128)S(1)} %add_divide_fusion), kind=kOutput, calls=%fused_computation.35 | convolution fusion | flops 67305472 | bytes 655376 | tf_op jit(solution)/shard_map/hrv,hrw->hvw/dot_general | solution.py:67
  34.2 0.4 %fusion.1 = bf16[4,512,128]{2,1,0:T(8,128)(2,1)S(1)} fusion(bf16[4,512,128]{2,1,0:T(8,128)(2,1)S(1)} %bitcast.27, bf16[4,128,128]{2,1,0:T(8,128)(2,1)S(1)} %fusion.20, f32[4]{0:T(128)S(1)} %add_divide_fusion), kind=kOutput, calls=%fused_computation.6 | convolution fusion | flops 85524480 | bytes 1179664 | tf_op jit(solution)/shard_map/hrv,hvw->hrw/dot_general | solution.py:73
  34.6 0.4 convolution_convert_fusion.3
  35.0 0.4 %fusion.2 = bf16[4,512,128]{2,1,0:T(8,128)(2,1)S(1)} fusion(bf16[4,512,128]{2,1,0:T(8,128)(2,1)S(1)} %fusion.1, bf16[4,128,128]{2,1,0:T(8,128)(2,1)S(1)} %convolution_convert_fusion.3), kind=kOutput, calls=%fused_computation.7 | convolution fusion | flops 85262336 | bytes 1179648 | tf_op jit(solution)/shard_map/hrv,hvw->hrw/dot_general | solution.py:73
  35.4 0.3 convolution_convert_fusion.2
  35.8 0.4 %fusion.3 = bf16[4,512,128]{2,1,0:T(8,128)(2,1)S(1)} fusion(bf16[4,512,128]{2,1,0:T(8,128)(2,1)S(1)} %fusion.2, bf16[4,128,128]{2,1,0:T(8,128)(2,1)S(1)} %convolution_convert_fusion.2), kind=kOutput, calls=%fused_computation.8 | convolution fusion | flops 85262336 | bytes 1179648 | tf_op jit(solution)/shard_map/hrv,hvw->hrw/dot_general | solution.py:73
  36.2 0.3 convolution_convert_fusion.1
  36.6 0.4 %fusion.4 = bf16[4,512,128]{2,1,0:T(8,128)(2,1)S(1)} fusion(bf16[4,512,128]{2,1,0:T(8,128)(2,1)S(1)} %fusion.3, bf16[4,128,128]{2,1,0:T(8,128)(2,1)S(1)} %convolution_convert_fusion.1), kind=kOutput, calls=%fused_computation.9 | convolution fusion | flops 85262336 | bytes 1179648 | tf_op jit(solution)/shard_map/hrv,hvw->hrw/dot_general | solution.py:73
  37.0 0.3 convolution_convert_fusion
  37.3 1.2 %fusion.8 = bf16[4,512,128]{2,1,0:T(8,128)(2,1)} fusion(bf16[4,512,128]{2,1,0:T(8,128)(2,1)S(1)} %fusion.4, bf16[4,128,128]{2,1,0:T(8,128)(2,1)S(1)} %convolution_convert_fusion), kind=kOutput, calls=%fused_computation.13 | convolution fusion | flops 86048768 | bytes 1179648 | tf_op jit(solution)/shard_map/hrv,hvw->hrw/dot_general | solution.py:73
  (1 shorter events, 0.0 us)

commit v12 on v11

--- a/solution.py
+++ b/solution.py
@@ -296,10 +296,10 @@
         multiply_piece(i - 1)
         if i == TOKEN_PARTS:
             stage_gather(0)
+    stage_share(0)
     multiply_piece(len(pieces) - 1)
     for o in others:
         scatter_all(last, *o).start()
-    stage_share(0)
     stage_gather(1)
     reduce_all(last)
     stage_share(1)

time: 38.7 us -> 38.3 us (0.990)
  Pallas kernels: 33.5 us -> 33.1 us
    pallas_call x1, Pallas kernels: 33.5 us -> 33.1 us  [kernel_body(): pl.pallas_call(functools.partial(kernel, depth), out_shape=pltpu.VMEM((wi...]
where the time goes in v12:
time: 38.3 us; the launch traced here: 38.2 us
  Pallas kernels  33.1 us (86%)
  matrix products  4.79 us (13%)
    pallas_call x1, Pallas kernels, kernel_body(): pl.pallas_call(functools.partial(kernel, depth), out_shape=pltpu.VMEM((wi...  33.1 us
    dot_general x5, matrix products, newton_schulz(): jnp.einsum('hrv,hvw->hrw', ortho, poly, preferred_element_type=jnp.float32)  2.97 us
    dot_general x5, matrix products, newton_schulz(): jnp.einsum('hrv,hrw->hvw', ortho, ortho, preferred_element_type=jnp.float32)  1.82 us

profile of v12, /device:TPU:0, one launch (start us, length us, event | category | flops | bytes accessed | tf_op | source)
XLA Modules:
  0.0 38.2 jit_solution(7995108783669332752)
XLA Ops:
  0.0 33.1 %gradient_sums.1 = bf16[4,4,128,128]{3,2,1,0:T(8,128)(2,1)S(1)} custom-call(s32[8]{0:T(128)} %len_hbm.1, bf16[1536,128]{1,0:T(8,128)(2,1)} %lat_hbm.1, bf16[1536,512]{1,0:T(8,128)(2,1)} %vg_hbm.1), custom_call_target="tpu_custom_call" | custom-call | tf_op jit(solution)/shard_map/gradient_sums/pallas_call | solution.py:339
  33.1 0.2 multiply_reduce_fusion
  33.3 0.4 %fusion.20 = bf16[4,128,128]{2,1,0:T(8,128)(2,1)S(1)} fusion(bf16[4,512,128]{2,1,0:T(8,128)(2,1)S(1)} %bitcast.26, f32[4]{0:T(128)S(1)} %add_divide_fusion), kind=kOutput, calls=%fused_computation.35 | convolution fusion | flops 67305472 | bytes 655376 | tf_op jit(solution)/shard_map/hrv,hrw->hvw/dot_general | solution.py:67
  33.7 0.4 %fusion.1 = bf16[4,512,128]{2,1,0:T(8,128)(2,1)S(1)} fusion(bf16[4,512,128]{2,1,0:T(8,128)(2,1)S(1)} %bitcast.27, bf16[4,128,128]{2,1,0:T(8,128)(2,1)S(1)} %fusion.20, f32[4]{0:T(128)S(1)} %add_divide_fusion), kind=kOutput, calls=%fused_computation.6 | convolution fusion | flops 85524480 | bytes 1179664 | tf_op jit(solution)/shard_map/hrv,hvw->hrw/dot_general | solution.py:73
  34.2 0.4 convolution_convert_fusion.3
  34.5 0.4 %fusion.2 = bf16[4,512,128]{2,1,0:T(8,128)(2,1)S(1)} fusion(bf16[4,512,128]{2,1,0:T(8,128)(2,1)S(1)} %fusion.1, bf16[4,128,128]{2,1,0:T(8,128)(2,1)S(1)} %convolution_convert_fusion.3), kind=kOutput, calls=%fused_computation.7 | convolution fusion | flops 85262336 | bytes 1179648 | tf_op jit(solution)/shard_map/hrv,hvw->hrw/dot_general | solution.py:73
  35.0 0.4 convolution_convert_fusion.2
  35.3 0.4 %fusion.3 = bf16[4,512,128]{2,1,0:T(8,128)(2,1)S(1)} fusion(bf16[4,512,128]{2,1,0:T(8,128)(2,1)S(1)} %fusion.2, bf16[4,128,128]{2,1,0:T(8,128)(2,1)S(1)} %convolution_convert_fusion.2), kind=kOutput, calls=%fused_computation.8 | convolution fusion | flops 85262336 | bytes 1179648 | tf_op jit(solution)/shard_map/hrv,hvw->hrw/dot_general | solution.py:73
  35.8 0.4 convolution_convert_fusion.1
  36.1 0.4 %fusion.4 = bf16[4,512,128]{2,1,0:T(8,128)(2,1)S(1)} fusion(bf16[4,512,128]{2,1,0:T(8,128)(2,1)S(1)} %fusion.3, bf16[4,128,128]{2,1,0:T(8,128)(2,1)S(1)} %convolution_convert_fusion.1), kind=kOutput, calls=%fused_computation.9 | convolution fusion | flops 85262336 | bytes 1179648 | tf_op jit(solution)/shard_map/hrv,hvw->hrw/dot_general | solution.py:73
  36.6 0.4 convolution_convert_fusion
  36.9 1.2 %fusion.8 = bf16[4,512,128]{2,1,0:T(8,128)(2,1)} fusion(bf16[4,512,128]{2,1,0:T(8,128)(2,1)S(1)} %fusion.4, bf16[4,128,128]{2,1,0:T(8,128)(2,1)S(1)} %convolution_convert_fusion), kind=kOutput, calls=%fused_computation.13 | convolution fusion | flops 86048768 | bytes 1179648 | tf_op jit(solution)/shard_map/hrv,hvw->hrw/dot_general | solution.py:73
  (1 shorter events, 0.0 us)
